TPU v7x, 128 devices: a whole 4x4x4 slice. The times are simulated.
128 devices in a mesh: dom: 16 (over y, z), sub: 8 (over x, core).
Axes of the slice: x: 4, y: 4, z: 4, core: 2. Of those that a mesh axis runs over, the one named last changes fastest.
Arguments:
- fine_latent: bfloat16 [4096, 64, 128], P(('dom', 'sub')), may hold values from -6 to 6
- coarse_latent: bfloat16 [1024, 64, 128], P(('dom', 'sub')), may hold values from -6 to 6
- adj_index: int32 [4096, 16], P(('dom', 'sub')), may hold values from 0 to 79
- adj_weight: bfloat16 [4096, 64, 1024], P(('dom', 'sub')), may hold values from -0.1875 to 0.1875
- interp_slot: int32 [4096, 4], P(('dom', 'sub')), may hold values from 0 to 127
- interp_weight: bfloat16 [4096, 64, 256], P(('dom', 'sub')), may hold values from -0.375 to 0.375
- coarse_send: int32 [128, 128, 1], P(('dom', 'sub')), may hold values from 0 to 7
- halo_sub_send: int32 [128, 8, 4], P(('dom', 'sub')), may hold values from 0 to 31
- halo_dom_send: int32 [128, 2, 8], P(('dom', 'sub')), may hold values from 0 to 31
- block_count: int32 [128], P(('dom', 'sub')), may hold values from 16 to 32, as said below
- w_in: bfloat16 [2, 384, 128], replicated, may hold values from -0.3125 to 0.3125
- b_in: float32 [2, 128], replicated, may hold values from -3 to 3
- w_out: bfloat16 [2, 128, 128], replicated, may hold values from -0.5 to 0.5
- ln_gain: float32 [2, 128], replicated, may hold values from 0.25 to 1.75
Outputs:
- fine_out: bfloat16 [4096, 64, 128], P(('dom', 'sub'))
Inputs may be any that keep to these rules, and one draw needn't show every extreme that they name: `block_count`: some device has all 32 blocks live and some has half of them.
All inputs are finite; a program needn't handle non-finite values.
Results may differ from a plain program's by a relative error of at most 0.0058.
Values may be sent and summed in bfloat16 or wider, within the bound.
No kernel may reach another device: no remote copies, remote signals or barrier semaphores. Data moves between devices by JAX's collectives and lax.ppermute only.
A program may use at most 64 MiB of HBM per device.

v0:
```python
import functools

import jax
import jax.numpy as jnp
from jax import lax
from jax.experimental import pallas as pl
from jax.experimental.pallas import tpu as pltpu
from jax.sharding import PartitionSpec as P

BF16 = jnp.bfloat16
F32 = jnp.float32
SMEM = pl.BlockSpec(memory_space=pltpu.SMEM)
VMEM = pl.BlockSpec(memory_space=pltpu.VMEM)
ANY = pl.BlockSpec(memory_space=pl.ANY)
CORES = 2


def in_hbm(array):
    return pltpu.with_memory_space_constraint(array, pltpu.HBM)


def in_vmem(array):
    return pltpu.with_memory_space_constraint(array, pltpu.VMEM)


def params(mib):
    return pltpu.CompilerParams(vmem_limit_bytes=mib << 20)


def blocks_like(count, latent):
    return jax.ShapeDtypeStruct((count,) + latent.shape[1:], BF16)


def chunked(source, target, sems):
    parts = sems.shape[0]
    size = source.shape[0] // parts
    return [
        pltpu.make_async_copy(
            source.at[pl.ds(part * size, size)], target.at[pl.ds(part * size, size)], sems.at[part]
        )
        for part in range(parts)
    ]


def start(copies):
    for copy in copies:
        copy.start()


def wait(copies):
    for copy in copies:
        copy.wait()


def copy_for_other_core(latent, sub_ids, out):
    slots, peers = sub_ids.shape
    me = lax.axis_index("sub")
    for way in range(peers // CORES):
        peer = me ^ (way * CORES + 1)
        for slot in range(slots):
            out[way * slots + slot] = latent[sub_ids[slot, peer]]


def copy_for_dom(latent, dom_ids, way, out):
    for slot in range(dom_ids.shape[1]):
        out[slot] = latent[dom_ids[way, slot]]


def copy_for_x(latent, sub_ids, passed, outs):
    slots = sub_ids.shape[0]
    me = lax.axis_index("sub")
    mine = (me % CORES) * slots
    for way, out in enumerate(outs, 1):
        for slot in range(slots):
            out[mine + slot] = latent[sub_ids[slot, me ^ (way * CORES)]]
            out[slots - mine + slot] = passed[way * slots + slot]


def first_hop_kernel(sub_ids, latent, after, other, sems):
    del after
    slots, peers = sub_ids.shape
    me = lax.axis_index("sub")
    copies = []
    for way in range(peers // CORES):
        peer = me ^ (way * CORES + 1)
        for slot in range(slots):
            place = way * slots + slot
            copies.append(
                pltpu.make_async_copy(
                    latent.at[sub_ids[slot, peer]], other.at[place], sems.at[place]
                )
            )
    start(copies)
    wait(copies)


def first_hop(latent, sub_ids, after):
    count = sub_ids.size // CORES
    return pl.pallas_call(
        first_hop_kernel,
        in_specs=[SMEM, ANY, ANY],
        out_specs=VMEM,
        out_shape=blocks_like(count, latent),
        scratch_shapes=[pltpu.SemaphoreType.DMA((count,))],
        compiler_params=params(8),
        name="first_hop",
    )(*map(in_hbm, (sub_ids, latent, after)))


def x_counts(sub_ids):
    slots, peers = sub_ids.shape
    return [slots * CORES] * (peers // CORES - 1)


def pick_kernel(ids, table, out, staged, sems):
    copies = chunked(staged, out, sems)
    size = staged.shape[0] // len(copies)
    for part, copy in enumerate(copies):
        for slot in range(part * size, (part + 1) * size):
            staged[slot] = table[ids[0, slot]]
        copy.start()
    wait(copies)


def pick(coarse, ids):
    shape = (ids.shape[1],) + coarse.shape[1:]
    return pl.pallas_call(
        pick_kernel,
        in_specs=[SMEM, VMEM],
        out_specs=ANY,
        out_shape=pltpu.HBM(shape, BF16),
        scratch_shapes=[pltpu.VMEM(shape, BF16), pltpu.SemaphoreType.DMA((8,))],
        compiler_params=params(8),
        name="pick",
    )(in_hbm(ids), in_hbm(coarse))


def repack_kernel(sub_ids, dom_ids, latent, passed, *outs):
    *pieces, up, down = outs
    copy_for_x(latent, sub_ids, passed, pieces)
    copy_for_dom(latent, dom_ids, 0, up)
    copy_for_dom(latent, dom_ids, 1, down)


def repack(latent, passed, sub_ids, dom_ids):
    counts = x_counts(sub_ids) + [dom_ids.shape[1]] * 2
    return pl.pallas_call(
        repack_kernel,
        in_specs=[SMEM, SMEM, VMEM, VMEM],
        out_specs=[VMEM] * len(counts),
        out_shape=[blocks_like(count, latent) for count in counts],
        compiler_params=params(8),
        name="repack",
    )(sub_ids, dom_ids, latent, passed)


def second_hop(latent, passed, sub_ids, dom_ids):
    *pieces, up, down = repack(latent, passed, sub_ids, dom_ids)
    pieces = along_x(pieces)
    return passed, pieces, along_dom(up, 1), along_dom(down, -1)


def to_other_core(blocks):
    return lax.ppermute(blocks, "sub", [(i, i ^ 1) for i in range(lax.axis_size("sub"))])


def along_x(pieces):
    size = lax.axis_size("sub")
    return [
        lax.ppermute(piece, "sub", [(i, i ^ (way * CORES)) for i in range(size)])
        for way, piece in enumerate(pieces, 1)
    ]


def along_dom(blocks, distance):
    devices = range(lax.axis_size("dom"))
    route = [(i, i + distance) for i in devices if i + distance in devices]
    return lax.ppermute(blocks, "dom", route)


def pool_copies(pool, sems, latent, sub_ids, passed, below, above, pieces):
    slots, peers = sub_ids.shape
    own = latent.shape[0]
    me = lax.axis_index("sub")
    places = [(latent, 0), (passed.at[pl.ds(0, slots)], own + (me ^ 1) * slots)]
    for way, piece in enumerate(pieces, 1):
        places.append((piece, own + (me // CORES ^ way) * CORES * slots))
    end = own + peers * slots
    places += [(below, end), (above, end + below.shape[0])]
    return [
        pltpu.make_async_copy(part, pool.at[pl.ds(first, part.shape[0])], sems.at[position])
        for position, (part, first) in enumerate(places)
    ]


def copy_to_self(pool, sub_ids, own):
    slots = sub_ids.shape[0]
    me = lax.axis_index("sub")
    for slot in range(slots):
        pool[own + me * slots + slot] = pool[sub_ids[slot, me]]


def tile_product(weights, table, ids, block, width):
    total = None
    rows = table.shape[1]
    for first in range(0, ids.shape[0], width):
        gathered = jnp.concatenate(
            [table[ids[first + tile, block]] for tile in range(width)], axis=0
        )
        part = jnp.dot(
            weights[block, :, first * rows : (first + width) * rows],
            gathered,
            preferred_element_type=F32,
        )
        total = part if total is None else total + part
    return total.astype(BF16)


def products(weights, table, ids, out, first, last):
    rows = table.shape[1]
    for block in range(first, last):
        out[pl.ds(block * rows, rows)] = tile_product(weights, table, ids, block, 4)


def node_network(latent, summed, interp, w_in, b_in, w_out, gain, live):
    joined = jnp.concatenate([latent, summed, interp], axis=1)
    hidden = jnp.dot(joined, w_in, preferred_element_type=F32) + b_in
    hidden = jnp.maximum(hidden, 0.0).astype(BF16)
    out = jnp.dot(hidden, w_out, preferred_element_type=F32)
    average = jnp.mean(out, axis=-1, keepdims=True)
    centred = out - average
    variance = jnp.mean(centred * centred, axis=-1, keepdims=True)
    normed = centred * lax.rsqrt(variance + 1e-05) * gain
    updated = latent.astype(F32) + normed
    return jnp.where(live, updated, 0.0).astype(BF16)


def step_blocks(t, pool, summed, interp, w_in, b_in, w_out, gain, count, first, last):
    rows, lat = pool.shape[1:]
    size = (last - first) * rows
    here = pl.ds(first * rows, size)
    index = first * rows + lax.broadcasted_iota(jnp.int32, (size, 1), 0)
    new = node_network(
        pool[pl.ds(first, last - first)].reshape(size, lat),
        summed[here],
        interp[here],
        w_in[t],
        b_in[t : t + 1],
        w_out[t],
        gain[t : t + 1],
        index < count * rows,
    )
    return new.reshape(last - first, rows, lat)


def first_kernel(
    ids, sub_ids, count, slots, received, weights, interp_weights, w_in, b_in, w_out, gain,
    latent, passed, *rest,
):
    ways = sub_ids.shape[1] // CORES - 1
    pieces, (below, above, *rest) = rest[:ways], rest[ways:]
    new, other, interp, held, pool, summed, coarse, slots_held, *net = rest
    net, sems = net[:4], net[4:]
    slot_sem, interp_sems, pool_sems, in_sems, network_sems = sems
    bring = pltpu.make_async_copy(slots, slots_held, slot_sem)
    bring.start()
    coarse_arriving = chunked(interp_weights, coarse, interp_sems)
    start(coarse_arriving)
    pools = pool_copies(pool, pool_sems, latent, sub_ids, passed, below, above, pieces)
    start(pools)
    network = [
        pltpu.make_async_copy(source, target, network_sems.at[position])
        for position, (source, target) in enumerate(zip((w_in, b_in, w_out, gain), net))
    ]
    start(network)
    arriving = chunked(weights, held, in_sems)
    start(arriving)
    bring.wait()
    blocks = held.shape[0]
    size = blocks // len(coarse_arriving)
    for part, copy in enumerate(coarse_arriving):
        copy.wait()
        products(coarse, received, slots_held, interp, part * size, (part + 1) * size)
    wait(pools)
    copy_to_self(pool, sub_ids, blocks)
    size = blocks // len(arriving)
    for part, copy in enumerate(arriving):
        copy.wait()
        products(held, pool, ids, summed, part * size, (part + 1) * size)
    wait(network)
    new[...] = step_blocks(0, pool, summed, interp, *net, count[0], 0, blocks)
    copy_for_other_core(new, sub_ids, other)


def first_step(
    received, slots, interp_weights, latent, halo, ids, weights, w_in, b_in, w_out, gain, count,
    sub_ids, dom_ids,
):
    blocks, rows, lat = latent.shape
    pool = blocks + sub_ids.size + dom_ids.size
    return pl.pallas_call(
        first_kernel,
        in_specs=[SMEM] * 3 + [ANY, VMEM] + [ANY] * (7 + len(halo)),
        out_specs=[VMEM] * 4,
        out_shape=[
            blocks_like(blocks, latent),
            blocks_like(sub_ids.size // CORES, latent),
            jax.ShapeDtypeStruct((blocks * rows, lat), BF16),
            pltpu.VMEM(weights.shape, BF16),
        ],
        scratch_shapes=[
            pltpu.VMEM((pool, rows, lat), BF16),
            pltpu.VMEM((blocks * rows, lat), BF16),
            pltpu.VMEM(interp_weights.shape, BF16),
            pltpu.SMEM(slots.shape, jnp.int32),
            *(pltpu.VMEM(part.shape, part.dtype) for part in (w_in, b_in, w_out, gain)),
            pltpu.SemaphoreType.DMA,
            pltpu.SemaphoreType.DMA((2,)),
            pltpu.SemaphoreType.DMA((1 + len(halo),)),
            pltpu.SemaphoreType.DMA((4,)),
            pltpu.SemaphoreType.DMA((4,)),
        ],
        compiler_params=params(16),
        name="first_step",
    )(
        ids, sub_ids, count, in_hbm(slots), received,
        *map(in_hbm, (weights, interp_weights, w_in, b_in, w_out, gain, latent)), *halo,
    )


def second_kernel(
    ids, sub_ids, count, weights, interp, w_in, b_in, w_out, gain, latent, passed, *rest,
):
    ways = sub_ids.shape[1] // CORES - 1
    pieces, (below, above, *rest) = rest[:ways], rest[ways:]
    out, pool, summed, staged, *net, pool_sems, network_sems, out_sems = rest
    pools = pool_copies(pool, pool_sems, latent, sub_ids, passed, below, above, pieces)
    start(pools)
    network = [
        pltpu.make_async_copy(source, target, network_sems.at[position])
        for position, (source, target) in enumerate(zip((w_in, b_in, w_out, gain), net))
    ]
    start(network)
    wait(pools)
    blocks = latent.shape[0]
    copy_to_self(pool, sub_ids, blocks)
    products(weights, pool, ids, summed, 0, blocks)
    wait(network)
    copies = chunked(staged, out, out_sems)
    size = blocks // len(copies)
    for part, copy in enumerate(copies):
        first, end = part * size, (part + 1) * size
        staged[pl.ds(first, size)] = step_blocks(
            1, pool, summed, interp, *net, count[0], first, end
        )
        copy.start()
    wait(copies)


def second_step(
    latent, halo, weights, interp, ids, w_in, b_in, w_out, gain, count, sub_ids, dom_ids
):
    blocks, rows, lat = latent.shape
    pool = blocks + sub_ids.size + dom_ids.size
    return pl.pallas_call(
        second_kernel,
        in_specs=[SMEM] * 3 + [VMEM, VMEM] + [ANY] * (5 + len(halo)),
        out_specs=ANY,
        out_shape=pltpu.HBM(latent.shape, BF16),
        scratch_shapes=[
            pltpu.VMEM((pool, rows, lat), BF16),
            pltpu.VMEM((blocks * rows, lat), BF16),
            pltpu.VMEM(latent.shape, BF16),
            *(pltpu.VMEM(part.shape, part.dtype) for part in (w_in, b_in, w_out, gain)),
            pltpu.SemaphoreType.DMA((1 + len(halo),)),
            pltpu.SemaphoreType.DMA((4,)),
            pltpu.SemaphoreType.DMA((2,)),
        ],
        compiler_params=params(16),
        name="second_step",
    )(
        ids, sub_ids, count, in_vmem(weights), interp, *map(in_hbm, (w_in, b_in, w_out, gain)),
        latent, *halo,
    )


def per_device(
    fine_latent,
    coarse_latent,
    adj_index,
    adj_weight,
    interp_slot,
    interp_weight,
    coarse_send,
    halo_sub_send,
    halo_dom_send,
    block_count,
    w_in,
    b_in,
    w_out,
    ln_gain,
):
    sub_ids = halo_sub_send[0].T
    dom_ids = halo_dom_send[0]
    adj_ids = adj_index.T
    payload = pick(coarse_latent, coarse_send.reshape(1, -1))
    received = lax.all_to_all(payload, ("dom", "sub"), split_axis=0, concat_axis=0, tiled=True)
    passed = to_other_core(first_hop(fine_latent, sub_ids, payload))
    passed, pieces, below, above = second_hop(fine_latent, passed, sub_ids, dom_ids)
    halo = [passed, *pieces, below, above]
    latent, other, interp, weights = first_step(
        received, interp_slot.T, interp_weight, fine_latent, halo, adj_ids, adj_weight, w_in, b_in,
        w_out, ln_gain, block_count, sub_ids, dom_ids,
    )
    passed = to_other_core(other)
    passed, pieces, below, above = second_hop(latent, passed, sub_ids, dom_ids)
    halo = [passed, *pieces, below, above]
    return second_step(
        latent, halo, weights, interp, adj_ids, w_in, b_in, w_out, ln_gain, block_count, sub_ids,
        dom_ids,
    )


def solution(mesh):
    split = ("dom", "sub")
    placed = (
        P(split, None, None),
        P(split, None, None),
        P(split, None),
        P(split, None, None),
        P(split, None),
        P(split, None, None),
        P(split, None, None),
        P(split, None, None),
        P(split, None, None),
        P(split),
        P(),
        P(),
        P(),
        P(),
    )
    return jax.shard_map(
        per_device,
        mesh=mesh,
        in_specs=placed,
        out_specs=P(split, None, None),
        check_vma=False,
    )
```

profile of v0, /device:TPU:0, one launch (start us, length us, event | category | flops | bytes accessed | tf_op | source)
XLA Modules:
  0.0 73.2 jit_solution(8333684751541208442)
XLA Ops:
  0.0 2.4 %pick.1.after = bf16[128,64,128]{2,1,0:T(8,128)(2,1)} custom-call(s32[1,128]{1,0:T(1,128)} %bitcast.17, bf16[8,64,128]{2,1,0:T(8,128)(2,1)} %table.1), custom_call_target="tpu_custom_call" | custom-call | tf_op jit(solution)/shard_map/pick/pallas_call | solution.py:127
  2.4 11.2 %all-to-all-start = ((bf16[128,64,128]{2,1,0:T(8,128)(2,1)}), bf16[128,64,128]{2,1,0:T(8,128)(2,1)S(1)}, u32[]{:S(2)}, u32[]{:S(2)}) async-start(bf16[128,64,128]{2,1,0:T(8,128)(2,1)} %pick.1.after), calls=%async_computation | async-start | bytes 4194304 | tf_op jit(solution)/shard_map/all_to_all | solution.py:407
  13.6 1.7 %first_hop.1 = bf16[16,64,128]{2,1,0:T(8,128)(2,1)S(1)} custom-call(s32[4,8]{1,0:T(4,128)} %bitcast.7, bf16[32,64,128]{2,1,0:T(8,128)(2,1)} %latent.5, bf16[128,64,128]{2,1,0:T(8,128)(2,1)} %pick.1.after), custom_call_target="tpu_custom_call" | custom-call | tf_op jit(solution)/shard_map/first_hop/pallas_call | solution.py:99
  15.3 0.1 collective-permute-start
  15.4 1.5 %collective-permute-done.passed = bf16[16,64,128]{2,1,0:T(8,128)(2,1)S(1)} collective-permute-done((bf16[16,64,128]{2,1,0:T(8,128)(2,1)S(1)}, bf16[16,64,128]{2,1,0:T(8,128)(2,1)S(1)}, u32[]{:S(2)}, u32[]{:S(2)}) %collective-permute-start) | collective-permute-done | bytes 262176 | tf_op jit(solution)/shard_map/ppermute | solution.py:164
  17.0 0.6 repack.2
  17.6 1.0 %collective-permute-start.1 = (bf16[8,64,128]{2,1,0:T(8,128)(2,1)S(1)}, bf16[8,64,128]{2,1,0:T(8,128)(2,1)S(1)}, u32[]{:S(2)}, u32[]{:S(2)}) collective-permute-start(bf16[8,64,128]{2,1,0:T(8,128)(2,1)S(1)} %get-tuple-element.19), channel_id=1, source_target_pairs={{0,2},{1,3},{2,0},{3,1},{4,6},{5,7},{6,4},{7,5},{8,10},{9,11},{10,... | collective-permute-start | bytes 393224 | tf_op jit(solution)/shard_map/ppermute | solution.py:170
  18.6 2.7 %collective-permute-start.2 = (bf16[8,64,128]{2,1,0:T(8,128)(2,1)S(1)}, bf16[8,64,128]{2,1,0:T(8,128)(2,1)S(1)}, u32[]{:S(2)}, u32[]{:S(2)}) collective-permute-start(bf16[8,64,128]{2,1,0:T(8,128)(2,1)S(1)} %get-tuple-element.20), channel_id=1, source_target_pairs={{0,4},{1,5},{2,6},{3,7},{4,0},{5,1},{6,2},{7,3},{8,12},{9,13},{10,... | collective-permute-start | bytes 393224 | tf_op jit(solution)/shard_map/ppermute | solution.py:170
  21.3 1.1 %collective-permute-start.3 = (bf16[8,64,128]{2,1,0:T(8,128)(2,1)S(1)}, bf16[8,64,128]{2,1,0:T(8,128)(2,1)S(1)}, u32[]{:S(2)}, u32[]{:S(2)}) collective-permute-start(bf16[8,64,128]{2,1,0:T(8,128)(2,1)S(1)} %get-tuple-element.21), channel_id=1, source_target_pairs={{0,6},{1,7},{2,4},{3,5},{4,2},{5,3},{6,0},{7,1},{8,14},{9,15},{10,... | collective-permute-start | bytes 393224 | tf_op jit(solution)/shard_map/ppermute | solution.py:170
  22.4 3.0 %collective-permute-start.4 = (bf16[8,64,128]{2,1,0:T(8,128)(2,1)S(1)}, bf16[8,64,128]{2,1,0:T(8,128)(2,1)S(1)}, u32[]{:S(2)}, u32[]{:S(2)}) collective-permute-start(bf16[8,64,128]{2,1,0:T(8,128)(2,1)S(1)} %get-tuple-element.22), channel_id=1, source_target_pairs={{0,8},{8,16},{16,24},{24,32},{32,40},{40,48},{48,56},{56,64},{64,7... | collective-permute-start | bytes 393224 | tf_op jit(solution)/shard_map/ppermute | solution.py:178
  25.4 1.3 %collective-permute-start.5 = (bf16[8,64,128]{2,1,0:T(8,128)(2,1)S(1)}, bf16[8,64,128]{2,1,0:T(8,128)(2,1)S(1)}, u32[]{:S(2)}, u32[]{:S(2)}) collective-permute-start(bf16[8,64,128]{2,1,0:T(8,128)(2,1)S(1)} %get-tuple-element.23), channel_id=1, source_target_pairs={{8,0},{16,8},{24,16},{32,24},{40,32},{48,40},{56,48},{64,56},{72,6... | collective-permute-start | bytes 393224 | tf_op jit(solution)/shard_map/ppermute | solution.py:178
  27.3 13.3 %collective-permute-done.1.rest_0_ = bf16[8,64,128]{2,1,0:T(8,128)(2,1)S(1)} collective-permute-done((bf16[8,64,128]{2,1,0:T(8,128)(2,1)S(1)}, bf16[8,64,128]{2,1,0:T(8,128)(2,1)S(1)}, u32[]{:S(2)}, u32[]{:S(2)}) %collective-permute-start.1) | collective-permute-done | bytes 131104 | tf_op jit(solution)/shard_map/ppermute | solution.py:170
  40.6 3.8 %collective-permute-done.2.rest_1_ = bf16[8,64,128]{2,1,0:T(8,128)(2,1)S(1)} collective-permute-done((bf16[8,64,128]{2,1,0:T(8,128)(2,1)S(1)}, bf16[8,64,128]{2,1,0:T(8,128)(2,1)S(1)}, u32[]{:S(2)}, u32[]{:S(2)}) %collective-permute-start.2) | collective-permute-done | bytes 131104 | tf_op jit(solution)/shard_map/ppermute | solution.py:170
  44.5 6.2 %first_step.1 = (bf16[32,64,128]{2,1,0:T(8,128)(2,1)S(1)}, bf16[16,64,128]{2,1,0:T(8,128)(2,1)S(1)}, bf16[2048,128]{1,0:T(8,128)(2,1)S(1)}, bf16[32,64,1024]{2,1,0:T(8,128)(2,1)S(1)}) custom-call(s32[16,32]{1,0:T(8,128)S(1)} %bitcast.12, s32[4,8]{1,0:T(4,128)S(1)} %bitcast.9, s32[1]{0:T(128)S(6)} %copy.15.count, s32[4,32]{1,0:T(4,128)} %bitcast.16, ...), custom_call_target="tpu_custom_call" | custom-call | tf_op jit(solution)/shard_map/first_step/pallas_call | solution.py:301
  50.8 1.5 %collective-permute-done.6.passed = bf16[16,64,128]{2,1,0:T(8,128)(2,1)S(1)} collective-permute-done((bf16[16,64,128]{2,1,0:T(8,128)(2,1)S(1)}, bf16[16,64,128]{2,1,0:T(8,128)(2,1)S(1)}, u32[]{:S(2)}, u32[]{:S(2)}) %collective-permute-start.6) | collective-permute-done | bytes 262176 | tf_op jit(solution)/shard_map/ppermute | solution.py:164
  52.3 0.6 repack.3
  53.0 0.6 collective-permute-start.7
  53.6 2.1 %collective-permute-start.8 = (bf16[8,64,128]{2,1,0:T(8,128)(2,1)S(1)}, bf16[8,64,128]{2,1,0:T(8,128)(2,1)S(1)}, u32[]{:S(2)}, u32[]{:S(2)}) collective-permute-start(bf16[8,64,128]{2,1,0:T(8,128)(2,1)S(1)} %get-tuple-element.29), channel_id=1, source_target_pairs={{0,4},{1,5},{2,6},{3,7},{4,0},{5,1},{6,2},{7,3},{8,12},{9,13},{10,... | collective-permute-start | bytes 393224 | tf_op jit(solution)/shard_map/ppermute | solution.py:170
  55.7 2.1 %collective-permute-start.9 = (bf16[8,64,128]{2,1,0:T(8,128)(2,1)S(1)}, bf16[8,64,128]{2,1,0:T(8,128)(2,1)S(1)}, u32[]{:S(2)}, u32[]{:S(2)}) collective-permute-start(bf16[8,64,128]{2,1,0:T(8,128)(2,1)S(1)} %get-tuple-element.30), channel_id=1, source_target_pairs={{0,6},{1,7},{2,4},{3,5},{4,2},{5,3},{6,0},{7,1},{8,14},{9,15},{10,... | collective-permute-start | bytes 393224 | tf_op jit(solution)/shard_map/ppermute | solution.py:170
  57.8 3.5 %collective-permute-start.10 = (bf16[8,64,128]{2,1,0:T(8,128)(2,1)S(1)}, bf16[8,64,128]{2,1,0:T(8,128)(2,1)S(1)}, u32[]{:S(2)}, u32[]{:S(2)}) collective-permute-start(bf16[8,64,128]{2,1,0:T(8,128)(2,1)S(1)} %get-tuple-element.31), channel_id=1, source_target_pairs={{0,8},{8,16},{16,24},{24,32},{32,40},{40,48},{48,56},{56,64},{64,7... | collective-permute-start | bytes 393224 | tf_op jit(solution)/shard_map/ppermute | solution.py:178
  61.3 1.3 %collective-permute-start.11 = (bf16[8,64,128]{2,1,0:T(8,128)(2,1)S(1)}, bf16[8,64,128]{2,1,0:T(8,128)(2,1)S(1)}, u32[]{:S(2)}, u32[]{:S(2)}) collective-permute-start(bf16[8,64,128]{2,1,0:T(8,128)(2,1)S(1)} %get-tuple-element.32), channel_id=1, source_target_pairs={{8,0},{16,8},{24,16},{32,24},{40,32},{48,40},{56,48},{64,56},{72,6... | collective-permute-start | bytes 393224 | tf_op jit(solution)/shard_map/ppermute | solution.py:178
  62.6 1.7 %collective-permute-done.9.rest_2_ = bf16[8,64,128]{2,1,0:T(8,128)(2,1)S(1)} collective-permute-done((bf16[8,64,128]{2,1,0:T(8,128)(2,1)S(1)}, bf16[8,64,128]{2,1,0:T(8,128)(2,1)S(1)}, u32[]{:S(2)}, u32[]{:S(2)}) %collective-permute-start.9) | collective-permute-done | bytes 131104 | tf_op jit(solution)/shard_map/ppermute | solution.py:170
  64.4 3.8 %collective-permute-done.11.rest_4_ = bf16[8,64,128]{2,1,0:T(8,128)(2,1)S(1)} collective-permute-done((bf16[8,64,128]{2,1,0:T(8,128)(2,1)S(1)}, bf16[8,64,128]{2,1,0:T(8,128)(2,1)S(1)}, u32[]{:S(2)}, u32[]{:S(2)}) %collective-permute-start.11) | collective-permute-done | bytes 131104 | tf_op jit(solution)/shard_map/ppermute | solution.py:178
  68.2 5.1 %second_step.1 = bf16[32,64,128]{2,1,0:T(8,128)(2,1)} custom-call(s32[16,32]{1,0:T(8,128)S(1)} %bitcast.13, s32[4,8]{1,0:T(4,128)S(1)} %bitcast.11, s32[1]{0:T(128)S(6)} %copy.15.count, bf16[32,64,1024]{2,1,0:T(8,128)(2,1)S(1)} %get-tuple-element.24.weights, bf16[2048,128]{1,0:T(8,128)(2,1)S(1)} %get-tuple-element.25.interp, bf16[2,384,128]{2,1,0:T(8,128)(2,1)} %w_in.3, ...), custom_call_target="tpu_custom_call" | custom-call | tf_op jit(solution)/shard_map/second_step/pallas_call | solution.py:365
  (16 shorter events, 0.1 us)
Async XLA Ops:
  0.0 16.9 %copy-start = (bf16[32,64,128]{2,1,0:T(8,128)(2,1)S(1)}, bf16[32,64,128]{2,1,0:T(8,128)(2,1)}, u32[]{:S(2)}) copy-start(bf16[32,64,128]{2,1,0:T(8,128)(2,1)} %latent.5) | copy-start | bytes 1572868
  0.0 16.9 %copy-start.1 = (s32[1,8,4]{1,2,0:T(4,128)S(1)}, s32[1,8,4]{1,2,0:T(4,128)}, u32[]{:S(2)}) copy-start(s32[1,8,4]{1,2,0:T(4,128)} %param.21) | copy-start | bytes 388
  0.0 16.9 %copy-start.3 = (s32[1,2,8]{2,1,0:T(2,128)S(1)}, s32[1,2,8]{2,1,0:T(2,128)}, u32[]{:S(2)}) copy-start(s32[1,2,8]{2,1,0:T(2,128)} %param.22) | copy-start | bytes 196
  2.4 42.1 %copy-start.2 = (s32[32,16]{0,1:T(8,128)S(1)}, s32[32,16]{0,1:T(8,128)}, u32[]{:S(2)}) copy-start(s32[32,16]{0,1:T(8,128)} %param.16) | copy-start | bytes 6148
  2.4 42.1 %all-to-all-start = ((bf16[128,64,128]{2,1,0:T(8,128)(2,1)}), bf16[128,64,128]{2,1,0:T(8,128)(2,1)S(1)}, u32[]{:S(2)}, u32[]{:S(2)}) async-start(bf16[128,64,128]{2,1,0:T(8,128)(2,1)} %pick.1.after), calls=%async_computation | async-start | bytes 4194304 | tf_op jit(solution)/shard_map/all_to_all | solution.py:407
  15.3 1.6 %collective-permute-start = (bf16[16,64,128]{2,1,0:T(8,128)(2,1)S(1)}, bf16[16,64,128]{2,1,0:T(8,128)(2,1)S(1)}, u32[]{:S(2)}, u32[]{:S(2)}) collective-permute-start(bf16[16,64,128]{2,1,0:T(8,128)(2,1)S(1)} %first_hop.1), channel_id=1, source_target_pairs={{0,1},{1,0},{2,3},{3,2},{4,5},{5,4},{6,7},{7,6},{8,9},{9,8},{10,11... | collective-permute-start | bytes 786440 | tf_op jit(solution)/shard_map/ppermute | solution.py:164
  17.6 23.0 %collective-permute-start.1 = (bf16[8,64,128]{2,1,0:T(8,128)(2,1)S(1)}, bf16[8,64,128]{2,1,0:T(8,128)(2,1)S(1)}, u32[]{:S(2)}, u32[]{:S(2)}) collective-permute-start(bf16[8,64,128]{2,1,0:T(8,128)(2,1)S(1)} %get-tuple-element.19), channel_id=1, source_target_pairs={{0,2},{1,3},{2,0},{3,1},{4,6},{5,7},{6,4},{7,5},{8,10},{9,11},{10,... | collective-permute-start | bytes 393224 | tf_op jit(solution)/shard_map/ppermute | solution.py:170
  18.6 25.8 %collective-permute-start.2 = (bf16[8,64,128]{2,1,0:T(8,128)(2,1)S(1)}, bf16[8,64,128]{2,1,0:T(8,128)(2,1)S(1)}, u32[]{:S(2)}, u32[]{:S(2)}) collective-permute-start(bf16[8,64,128]{2,1,0:T(8,128)(2,1)S(1)} %get-tuple-element.20), channel_id=1, source_target_pairs={{0,4},{1,5},{2,6},{3,7},{4,0},{5,1},{6,2},{7,3},{8,12},{9,13},{10,... | collective-permute-start | bytes 393224 | tf_op jit(solution)/shard_map/ppermute | solution.py:170
  21.3 23.2 %collective-permute-start.3 = (bf16[8,64,128]{2,1,0:T(8,128)(2,1)S(1)}, bf16[8,64,128]{2,1,0:T(8,128)(2,1)S(1)}, u32[]{:S(2)}, u32[]{:S(2)}) collective-permute-start(bf16[8,64,128]{2,1,0:T(8,128)(2,1)S(1)} %get-tuple-element.21), channel_id=1, source_target_pairs={{0,6},{1,7},{2,4},{3,5},{4,2},{5,3},{6,0},{7,1},{8,14},{9,15},{10,... | collective-permute-start | bytes 393224 | tf_op jit(solution)/shard_map/ppermute | solution.py:170
  22.4 22.1 %collective-permute-start.4 = (bf16[8,64,128]{2,1,0:T(8,128)(2,1)S(1)}, bf16[8,64,128]{2,1,0:T(8,128)(2,1)S(1)}, u32[]{:S(2)}, u32[]{:S(2)}) collective-permute-start(bf16[8,64,128]{2,1,0:T(8,128)(2,1)S(1)} %get-tuple-element.22), channel_id=1, source_target_pairs={{0,8},{8,16},{16,24},{24,32},{32,40},{40,48},{48,56},{56,64},{64,7... | collective-permute-start | bytes 393224 | tf_op jit(solution)/shard_map/ppermute | solution.py:178
  25.4 19.1 %collective-permute-start.5 = (bf16[8,64,128]{2,1,0:T(8,128)(2,1)S(1)}, bf16[8,64,128]{2,1,0:T(8,128)(2,1)S(1)}, u32[]{:S(2)}, u32[]{:S(2)}) collective-permute-start(bf16[8,64,128]{2,1,0:T(8,128)(2,1)S(1)} %get-tuple-element.23), channel_id=1, source_target_pairs={{8,0},{16,8},{24,16},{32,24},{40,32},{48,40},{56,48},{64,56},{72,6... | collective-permute-start | bytes 393224 | tf_op jit(solution)/shard_map/ppermute | solution.py:178
  50.7 1.6 %collective-permute-start.6 = (bf16[16,64,128]{2,1,0:T(8,128)(2,1)S(1)}, bf16[16,64,128]{2,1,0:T(8,128)(2,1)S(1)}, u32[]{:S(2)}, u32[]{:S(2)}) collective-permute-start(bf16[16,64,128]{2,1,0:T(8,128)(2,1)S(1)} %get-tuple-element.27), channel_id=1, source_target_pairs={{0,1},{1,0},{2,3},{3,2},{4,5},{5,4},{6,7},{7,6},{8,9},{9,8},{10,11... | collective-permute-start | bytes 786440 | tf_op jit(solution)/shard_map/ppermute | solution.py:164
  53.0 9.6 %collective-permute-start.7 = (bf16[8,64,128]{2,1,0:T(8,128)(2,1)S(1)}, bf16[8,64,128]{2,1,0:T(8,128)(2,1)S(1)}, u32[]{:S(2)}, u32[]{:S(2)}) collective-permute-start(bf16[8,64,128]{2,1,0:T(8,128)(2,1)S(1)} %get-tuple-element.28), channel_id=1, source_target_pairs={{0,2},{1,3},{2,0},{3,1},{4,6},{5,7},{6,4},{7,5},{8,10},{9,11},{10,... | collective-permute-start | bytes 393224 | tf_op jit(solution)/shard_map/ppermute | solution.py:170
  53.6 9.0 %collective-permute-start.8 = (bf16[8,64,128]{2,1,0:T(8,128)(2,1)S(1)}, bf16[8,64,128]{2,1,0:T(8,128)(2,1)S(1)}, u32[]{:S(2)}, u32[]{:S(2)}) collective-permute-start(bf16[8,64,128]{2,1,0:T(8,128)(2,1)S(1)} %get-tuple-element.29), channel_id=1, source_target_pairs={{0,4},{1,5},{2,6},{3,7},{4,0},{5,1},{6,2},{7,3},{8,12},{9,13},{10,... | collective-permute-start | bytes 393224 | tf_op jit(solution)/shard_map/ppermute | solution.py:170
  55.7 8.7 %collective-permute-start.9 = (bf16[8,64,128]{2,1,0:T(8,128)(2,1)S(1)}, bf16[8,64,128]{2,1,0:T(8,128)(2,1)S(1)}, u32[]{:S(2)}, u32[]{:S(2)}) collective-permute-start(bf16[8,64,128]{2,1,0:T(8,128)(2,1)S(1)} %get-tuple-element.30), channel_id=1, source_target_pairs={{0,6},{1,7},{2,4},{3,5},{4,2},{5,3},{6,0},{7,1},{8,14},{9,15},{10,... | collective-permute-start | bytes 393224 | tf_op jit(solution)/shard_map/ppermute | solution.py:170
  57.8 6.6 %collective-permute-start.10 = (bf16[8,64,128]{2,1,0:T(8,128)(2,1)S(1)}, bf16[8,64,128]{2,1,0:T(8,128)(2,1)S(1)}, u32[]{:S(2)}, u32[]{:S(2)}) collective-permute-start(bf16[8,64,128]{2,1,0:T(8,128)(2,1)S(1)} %get-tuple-element.31), channel_id=1, source_target_pairs={{0,8},{8,16},{16,24},{24,32},{32,40},{40,48},{48,56},{56,64},{64,7... | collective-permute-start | bytes 393224 | tf_op jit(solution)/shard_map/ppermute | solution.py:178
  61.3 6.9 %collective-permute-start.11 = (bf16[8,64,128]{2,1,0:T(8,128)(2,1)S(1)}, bf16[8,64,128]{2,1,0:T(8,128)(2,1)S(1)}, u32[]{:S(2)}, u32[]{:S(2)}) collective-permute-start(bf16[8,64,128]{2,1,0:T(8,128)(2,1)S(1)} %get-tuple-element.32), channel_id=1, source_target_pairs={{8,0},{16,8},{24,16},{32,24},{40,32},{48,40},{56,48},{64,56},{72,6... | collective-permute-start | bytes 393224 | tf_op jit(solution)/shard_map/ppermute | solution.py:178
where the time goes:
time: 74.3 us; the launch traced here: 73.2 us
  starting transfers between devices  30 us (40%)
  waiting for transfers between devices  25.8 us (35%)
  Pallas kernels  16.7 us (22%)
  between operations  0.8 us (1%)
    ppermute x6, waiting for transfers between devices, along_x(): lax.ppermute(piece, 'sub', [(i, i ^ way * CORES) for i in range(size)])  18.9 us
    all_to_all x1, starting transfers between devices, per_device(): lax.all_to_all(payload, ('dom', 'sub'), split_axis=0, concat_axis=0, tile...  11.2 us
    ppermute x6, starting transfers between devices, along_x(): lax.ppermute(piece, 'sub', [(i, i ^ way * CORES) for i in range(size)])  9.56 us
    ppermute x4, starting transfers between devices, along_dom(): return lax.ppermute(blocks, 'dom', route)  9.08 us
    pallas_call x1, Pallas kernels, first_step(): pl.pallas_call(first_kernel, in_specs=[SMEM] * 3 + [ANY, VMEM] + [ANY] *...  6.21 us
    pallas_call x1, Pallas kernels, second_step(): pl.pallas_call(second_kernel, in_specs=[SMEM] * 3 + [VMEM, VMEM] + [ANY]...  5.08 us
    ppermute x4, waiting for transfers between devices, along_dom(): return lax.ppermute(blocks, 'dom', route)  3.8 us
    ppermute x2, waiting for transfers between devices, to_other_core(): lax.ppermute(blocks, 'sub', [(i, i ^ 1) for i in range(lax.axis_size('sub...  3.04 us
  transfers between devices with their start and end apart: 13, of which 6 were waited for; matrix products, arithmetic and copies ran while one was open for 0% of the time, Pallas kernels for 3%

commit v1 on v0

v1 whole, which is shorter than its diff:
```python
import functools

import jax
import jax.numpy as jnp
from jax import lax
from jax.experimental import pallas as pl
from jax.experimental.pallas import tpu as pltpu
from jax.sharding import PartitionSpec as P

BF16 = jnp.bfloat16
F32 = jnp.float32
SMEM = pl.BlockSpec(memory_space=pltpu.SMEM)
VMEM = pl.BlockSpec(memory_space=pltpu.VMEM)
ANY = pl.BlockSpec(memory_space=pl.ANY)
CORES = 2
AHEAD = 2


def in_hbm(array):
    return pltpu.with_memory_space_constraint(array, pltpu.HBM)


def in_vmem(array):
    return pltpu.with_memory_space_constraint(array, pltpu.VMEM)


def params(mib):
    return pltpu.CompilerParams(vmem_limit_bytes=mib << 20)


def blocks_like(count, latent):
    return jax.ShapeDtypeStruct((count,) + latent.shape[1:], BF16)


def chunked(source, target, sems):
    parts = sems.shape[0]
    size = source.shape[0] // parts
    return [
        pltpu.make_async_copy(
            source.at[pl.ds(part * size, size)], target.at[pl.ds(part * size, size)], sems.at[part]
        )
        for part in range(parts)
    ]


def start(copies):
    for copy in copies:
        copy.start()


def wait(copies):
    for copy in copies:
        copy.wait()


def copy_for_other_core(latent, sub_ids, out):
    slots, peers = sub_ids.shape
    me = lax.axis_index("sub")
    for way in range(peers // CORES):
        peer = me ^ (way * CORES + 1)
        for slot in range(slots):
            out[way * slots + slot] = latent[sub_ids[slot, peer]]


def copy_for_dom(latent, dom_ids, way, out):
    for slot in range(dom_ids.shape[1]):
        out[slot] = latent[dom_ids[way, slot]]


def copy_for_x(latent, sub_ids, passed, outs):
    slots = sub_ids.shape[0]
    me = lax.axis_index("sub")
    mine = (me % CORES) * slots
    for way, out in enumerate(outs, 1):
        for slot in range(slots):
            out[mine + slot] = latent[sub_ids[slot, me ^ (way * CORES)]]
            out[slots - mine + slot] = passed[way * slots + slot]


def first_hop_kernel(sub_ids, latent, after, other, sems):
    del after
    slots, peers = sub_ids.shape
    me = lax.axis_index("sub")
    copies = []
    for way in range(peers // CORES):
        peer = me ^ (way * CORES + 1)
        for slot in range(slots):
            place = way * slots + slot
            copies.append(
                pltpu.make_async_copy(
                    latent.at[sub_ids[slot, peer]], other.at[place], sems.at[place]
                )
            )
    start(copies)
    wait(copies)


def first_hop(latent, sub_ids, after):
    count = sub_ids.size // CORES
    return pl.pallas_call(
        first_hop_kernel,
        in_specs=[SMEM, ANY, ANY],
        out_specs=VMEM,
        out_shape=blocks_like(count, latent),
        scratch_shapes=[pltpu.SemaphoreType.DMA((count,))],
        compiler_params=params(8),
        name="first_hop",
    )(*map(in_hbm, (sub_ids, latent, after)))


def x_counts(sub_ids):
    slots, peers = sub_ids.shape
    return [slots * CORES] * (peers // CORES - 1)


def pick_kernel(ids, table, out, ids_held, held, staged, load_sems, sems):
    loads = [
        pltpu.make_async_copy(ids, ids_held, load_sems.at[0]),
        pltpu.make_async_copy(table, held, load_sems.at[1]),
    ]
    start(loads)
    wait(loads)
    copies = chunked(staged, out, sems)
    size = staged.shape[0] // len(copies)
    for part, copy in enumerate(copies):
        for slot in range(part * size, (part + 1) * size):
            staged[slot] = held[ids_held[0, slot]]
        copy.start()
    wait(copies)


def pick(coarse, ids):
    shape = (ids.shape[1],) + coarse.shape[1:]
    return pl.pallas_call(
        pick_kernel,
        in_specs=[ANY, ANY],
        out_specs=ANY,
        out_shape=pltpu.HBM(shape, BF16),
        scratch_shapes=[
            pltpu.SMEM(ids.shape, jnp.int32),
            pltpu.VMEM(coarse.shape, BF16),
            pltpu.VMEM(shape, BF16),
            pltpu.SemaphoreType.DMA((2,)),
            pltpu.SemaphoreType.DMA((8,)),
        ],
        compiler_params=params(8),
        name="pick",
    )(in_hbm(ids), in_hbm(coarse))


def repack_kernel(sub_ids, dom_ids, latent, passed, *outs):
    *pieces, up, down = outs
    copy_for_x(latent, sub_ids, passed, pieces)
    copy_for_dom(latent, dom_ids, 0, up)
    copy_for_dom(latent, dom_ids, 1, down)


def repack(latent, passed, sub_ids, dom_ids):
    counts = x_counts(sub_ids) + [dom_ids.shape[1]] * 2
    return pl.pallas_call(
        repack_kernel,
        in_specs=[SMEM, SMEM, VMEM, VMEM],
        out_specs=[VMEM] * len(counts),
        out_shape=[blocks_like(count, latent) for count in counts],
        compiler_params=params(8),
        name="repack",
    )(sub_ids, dom_ids, latent, passed)


def to_other_core(blocks):
    return lax.ppermute(blocks, "sub", [(i, i ^ 1) for i in range(lax.axis_size("sub"))])


def along_x(pieces):
    size = lax.axis_size("sub")
    return [
        lax.ppermute(piece, "sub", [(i, i ^ (way * CORES)) for i in range(size)])
        for way, piece in enumerate(pieces, 1)
    ]


def along_dom(blocks, distance):
    size = lax.axis_size("dom")
    return lax.ppermute(blocks, "dom", [(i, (i + distance) % size) for i in range(size)])


def second_hop(latent, other, sub_ids, dom_ids):
    passed = to_other_core(other)
    *pieces, up, down = repack(latent, passed, sub_ids, dom_ids)
    return [passed, *along_x(pieces), along_dom(up, 1), along_dom(down, -1)]


def fill_pool(pool, own, sub_ids, passed, pieces, below, above):
    slots, peers = sub_ids.shape
    me = lax.axis_index("sub")
    pool[pl.ds(own + (me ^ 1) * slots, slots)] = passed[:slots]
    for way, piece in enumerate(pieces, 1):
        first = own + (me // CORES ^ way) * CORES * slots
        pool[pl.ds(first, piece.shape[0])] = piece[...]
    end = own + peers * slots
    pool[pl.ds(end, below.shape[0])] = below[...]
    pool[pl.ds(end + below.shape[0], above.shape[0])] = above[...]
    clear_ends(pool, below.shape[0])


def copy_to_self(pool, sub_ids, own):
    slots = sub_ids.shape[0]
    me = lax.axis_index("sub")
    for slot in range(slots):
        pool[own + me * slots + slot] = pool[sub_ids[slot, me]]


def clear_ends(pool, count):
    end = pool.shape[0]
    zeros = jnp.zeros((count,) + pool.shape[1:], pool.dtype)

    @pl.when(lax.axis_index("dom") == 0)
    def _():
        pool[pl.ds(end - 2 * count, count)] = zeros

    @pl.when(lax.axis_index("dom") == lax.axis_size("dom") - 1)
    def _():
        pool[pl.ds(end - count, count)] = zeros


def tile_product(weights, table, ids, block, width):
    total = None
    rows = table.shape[1]
    for first in range(0, ids.shape[0], width):
        gathered = jnp.concatenate(
            [table[ids[first + tile, block]] for tile in range(width)], axis=0
        )
        part = jnp.dot(
            weights[block, :, first * rows : (first + width) * rows],
            gathered,
            preferred_element_type=F32,
        )
        total = part if total is None else total + part
    return total.astype(BF16)


def products(weights, table, ids, out, first, last):
    rows = table.shape[1]
    for block in range(first, last):
        out[pl.ds(block * rows, rows)] = tile_product(weights, table, ids, block, 4)


def node_network(hidden, latent, w_out, gain, live):
    hidden = jnp.maximum(hidden, 0.0).astype(BF16)
    out = jnp.dot(hidden, w_out, preferred_element_type=F32)
    average = jnp.mean(out, axis=-1, keepdims=True)
    centred = out - average
    variance = jnp.mean(centred * centred, axis=-1, keepdims=True)
    normed = centred * lax.rsqrt(variance + 1e-05) * gain
    updated = latent.astype(F32) + normed
    return jnp.where(live, updated, 0.0).astype(BF16)


def live_rows(count, first, size):
    return first + lax.broadcasted_iota(jnp.int32, (size, 1), 0) < count


def first_kernel(
    count, ids, sub_ids, slots, received, weights, interp_weights, w_in, b_in, w_out, gain, latent,
    passed, *rest,
):
    ways = sub_ids.shape[1] // CORES - 1
    pieces, (below, above, *rest) = rest[:ways], rest[ways:]
    pool, other, interp, held, summed, coarse, *rest = rest
    tables, net, sems = rest[:3], rest[3:7], rest[7:]
    table_sems, interp_sems, own_sem, in_sems, network_sems = sems
    tabling = [
        pltpu.make_async_copy(source, target, table_sems.at[position])
        for position, (source, target) in enumerate(zip((slots, sub_ids, ids), tables))
    ]
    start(tabling)
    slots, sub_ids, ids = tables
    coarse_arriving = chunked(interp_weights, coarse, interp_sems)
    arriving = chunked(weights, held, in_sems)
    blocks, rows, lat = latent.shape
    bring = pltpu.make_async_copy(latent, pool.at[pl.ds(0, blocks)], own_sem)
    network = [
        pltpu.make_async_copy(source, target, network_sems.at[position])
        for position, (source, target) in enumerate(zip((w_in, b_in, w_out, gain), net))
    ]
    start(coarse_arriving)
    bring.start()
    queue = arriving + network
    start(queue[:AHEAD])
    queue = queue[AHEAD:]
    w_in, b_in, w_out, gain = net
    wait(tabling)
    fill_pool(pool, blocks, sub_ids, passed, pieces, below, above)
    size = blocks // len(coarse_arriving)
    for part, copy in enumerate(coarse_arriving):
        copy.wait()
        start(queue[:1])
        queue = queue[1:]
        products(coarse, received, slots, interp, part * size, (part + 1) * size)
    bring.wait()
    copy_to_self(pool, sub_ids, blocks)
    size = blocks // len(arriving)
    for part, copy in enumerate(arriving):
        copy.wait()
        start(queue[:2])
        queue = queue[2:]
        products(held, pool, ids, summed, part * size, (part + 1) * size)
    start(queue)
    wait(network)
    own = pool[pl.ds(0, blocks)].reshape(blocks * rows, lat)
    joined = jnp.concatenate([own, summed[...], interp[...]], axis=1)
    hidden = jnp.dot(joined, w_in[0], preferred_element_type=F32) + b_in[0:1]
    live = live_rows(count[0] * rows, 0, blocks * rows)
    new = node_network(hidden, own, w_out[0], gain[0:1], live)
    pool[pl.ds(0, blocks)] = new.reshape(blocks, rows, lat)
    copy_for_other_core(pool, sub_ids, other)
    copy_to_self(pool, sub_ids, blocks)


def first_step(
    received, slots, interp_weights, latent, halo, ids, weights, w_in, b_in, w_out, gain, count,
    sub_ids,
):
    blocks, rows, lat = latent.shape
    pool = blocks + sub_ids.size + 2 * halo[-1].shape[0]
    network = (w_in, b_in, w_out, gain)
    return pl.pallas_call(
        first_kernel,
        in_specs=[SMEM, ANY, ANY, ANY, VMEM] + [ANY] * 7 + [VMEM] * len(halo),
        out_specs=[VMEM] * 4,
        out_shape=[
            pltpu.VMEM((pool, rows, lat), BF16),
            blocks_like(sub_ids.size // CORES, latent),
            jax.ShapeDtypeStruct((blocks * rows, lat), BF16),
            pltpu.VMEM(weights.shape, BF16),
        ],
        scratch_shapes=[
            pltpu.VMEM((blocks * rows, lat), BF16),
            pltpu.VMEM(interp_weights.shape, BF16),
            *(pltpu.SMEM(part.shape, jnp.int32) for part in (slots, sub_ids, ids)),
            *(pltpu.VMEM(part.shape, part.dtype) for part in network),
            pltpu.SemaphoreType.DMA((3,)),
            pltpu.SemaphoreType.DMA((2,)),
            pltpu.SemaphoreType.DMA,
            pltpu.SemaphoreType.DMA((4,)),
            pltpu.SemaphoreType.DMA((4,)),
        ],
        compiler_params=params(16),
        name="first_step",
    )(
        count, *map(in_hbm, (ids, sub_ids, slots)), received,
        *map(in_hbm, (weights, interp_weights, *network, latent)), *halo,
    )


def second_kernel(
    ids, count, weights, interp, w_in, b_in, w_out, gain, pool_in, sub_shape, passed, *rest
):
    del pool_in
    ways = sub_shape.shape[1] // CORES - 1
    pieces, (below, above, *rest) = rest[:ways], rest[ways:]
    pool, out, summed, staged, out_sems = rest
    blocks, rows, lat = staged.shape
    fill_pool(pool, blocks, sub_shape, passed, pieces, below, above)
    products(weights, pool, ids, summed, 0, blocks)
    copies = chunked(staged, out, out_sems)
    size = blocks // len(copies)
    for part, copy in enumerate(copies):
        mine = pl.ds(part * size, size)
        here = pl.ds(part * size * rows, size * rows)
        own = pool[mine].reshape(size * rows, lat)
        joined = jnp.concatenate([own, summed[here], interp[here]], axis=1)
        hidden = jnp.dot(joined, w_in[1], preferred_element_type=F32) + b_in[1:2]
        live = live_rows(count[0] * rows, part * size * rows, size * rows)
        new = node_network(hidden, own, w_out[1], gain[1:2], live)
        staged[mine] = new.reshape(size, rows, lat)
        copy.start()
    wait(copies)


def second_step(pool, halo, weights, interp, ids, w_in, b_in, w_out, gain, count, sub_ids):
    rows, lat = pool.shape[1:]
    blocks = weights.shape[0]
    operands = [ids, count, in_vmem(weights), interp, w_in, b_in, w_out, gain, in_vmem(pool)]
    return pl.pallas_call(
        second_kernel,
        in_specs=[SMEM] * 2 + [VMEM] * 7 + [ANY] + [VMEM] * len(halo),
        out_specs=[VMEM, ANY],
        out_shape=[pltpu.VMEM(pool.shape, BF16), pltpu.HBM((blocks, rows, lat), BF16)],
        input_output_aliases={len(operands) - 1: 0},
        scratch_shapes=[
            pltpu.VMEM((blocks * rows, lat), BF16),
            pltpu.VMEM((blocks, rows, lat), BF16),
            pltpu.SemaphoreType.DMA((2,)),
        ],
        compiler_params=params(16),
        name="second_step",
    )(*operands, sub_ids, *halo)[1]


def per_device(
    fine_latent,
    coarse_latent,
    adj_index,
    adj_weight,
    interp_slot,
    interp_weight,
    coarse_send,
    halo_sub_send,
    halo_dom_send,
    block_count,
    w_in,
    b_in,
    w_out,
    ln_gain,
):
    sub_ids = halo_sub_send[0].T
    dom_ids = halo_dom_send[0]
    adj_ids = adj_index.T
    payload = pick(coarse_latent, coarse_send.reshape(1, -1))
    received = lax.all_to_all(payload, ("dom", "sub"), split_axis=0, concat_axis=0, tiled=True)
    halo = second_hop(fine_latent, first_hop(fine_latent, sub_ids, payload), sub_ids, dom_ids)
    pool, other, interp, weights = first_step(
        received, interp_slot.T, interp_weight, fine_latent, halo, adj_ids, adj_weight, w_in, b_in,
        w_out, ln_gain, block_count, sub_ids,
    )
    halo = second_hop(pool, other, sub_ids, dom_ids)
    return second_step(
        pool, halo, weights, interp, adj_ids, w_in, b_in, w_out, ln_gain, block_count, sub_ids
    )


def solution(mesh):
    split = ("dom", "sub")
    placed = (
        P(split, None, None),
        P(split, None, None),
        P(split, None),
        P(split, None, None),
        P(split, None),
        P(split, None, None),
        P(split, None, None),
        P(split, None, None),
        P(split, None, None),
        P(split),
        P(),
        P(),
        P(),
        P(),
    )
    return jax.shard_map(
        per_device,
        mesh=mesh,
        in_specs=placed,
        out_specs=P(split, None, None),
        check_vma=False,
    )
```

time: 74.3 us -> 69.7 us (0.938)
  waiting for transfers between devices: 25.8 us -> 21.9 us
  Pallas kernels: 16.7 us -> 14.5 us
  starting transfers between devices: 30 us -> 31.9 us
    ppermute x4, waiting for transfers between devices: 3.8 us -> 0.63 us  [along_dom(): lax.ppermute(blocks, 'dom', [(i, (i + distance) % size) for i in range(si...]
    pallas_call x3, Pallas kernels: 13.7 us -> 11.4 us  [the longest x1 5.14 us: first_step(): pl.pallas_call(first_kernel, in_specs=[SMEM, ANY, ANY, ANY, VMEM] + [ANY]...]
    ppermute x4, starting transfers between devices: 9.08 us -> 11 us  [along_dom(): lax.ppermute(blocks, 'dom', [(i, (i + distance) % size) for i in range(si...]
  transfers between devices with their start and end apart: 13 -> 13, of which waited for: 6 -> 7; matrix products, arithmetic and copies ran while one was open for 0% -> 0% of each run, Pallas kernels for 3% -> 4%
where the time goes in v1:
time: 69.7 us; the launch traced here: 69.3 us
  starting transfers between devices  31.9 us (46%)
  waiting for transfers between devices  21.9 us (31%)
  Pallas kernels  14.5 us (21%)
  between operations  0.84 us (1%)
    ppermute x6, waiting for transfers between devices, along_x(): lax.ppermute(piece, 'sub', [(i, i ^ way * CORES) for i in range(size)])  18.3 us
    all_to_all x1, starting transfers between devices, per_device(): lax.all_to_all(payload, ('dom', 'sub'), split_axis=0, concat_axis=0, tile...  11.1 us
    ppermute x4, starting transfers between devices, along_dom(): lax.ppermute(blocks, 'dom', [(i, (i + distance) % size) for i in range(si...  11 us
    ppermute x6, starting transfers between devices, along_x(): lax.ppermute(piece, 'sub', [(i, i ^ way * CORES) for i in range(size)])  9.56 us
    pallas_call x1, Pallas kernels, first_step(): pl.pallas_call(first_kernel, in_specs=[SMEM, ANY, ANY, ANY, VMEM] + [ANY]...  5.14 us
    pallas_call x1, Pallas kernels, second_step(): pl.pallas_call(second_kernel, in_specs=[SMEM] * 2 + [VMEM] * 7 + [ANY] +...  3.92 us
    ppermute x2, waiting for transfers between devices, to_other_core(): lax.ppermute(blocks, 'sub', [(i, i ^ 1) for i in range(lax.axis_size('sub...  3.04 us
    pallas_call x1, Pallas kernels, pick(): pl.pallas_call(pick_kernel, in_specs=[ANY, ANY], out_specs=ANY, out_shape...  2.34 us
  transfers between devices with their start and end apart: 13, of which 7 were waited for; matrix products, arithmetic and copies ran while one was open for 0% of the time, Pallas kernels for 4%

profile of v1, /device:TPU:0, one launch (start us, length us, event | category | flops | bytes accessed | tf_op | source)
XLA Modules:
  0.0 69.3 jit_solution(17747851919945639632)
XLA Ops:
  0.0 2.3 %pick.1.after = bf16[128,64,128]{2,1,0:T(8,128)(2,1)} custom-call(s32[1,128]{1,0:T(1,128)} %bitcast.17, bf16[8,64,128]{2,1,0:T(8,128)(2,1)} %table.1), custom_call_target="tpu_custom_call" | custom-call | tf_op jit(solution)/shard_map/pick/pallas_call | solution.py:134
  2.3 11.1 %all-to-all-start = ((bf16[128,64,128]{2,1,0:T(8,128)(2,1)}), bf16[128,64,128]{2,1,0:T(8,128)(2,1)S(1)}, u32[]{:S(2)}, u32[]{:S(2)}) async-start(bf16[128,64,128]{2,1,0:T(8,128)(2,1)} %pick.1.after), calls=%async_computation | async-start | bytes 4194304 | tf_op jit(solution)/shard_map/all_to_all | solution.py:421
  13.5 1.9 %first_hop.1 = bf16[16,64,128]{2,1,0:T(8,128)(2,1)S(1)} custom-call(s32[4,8]{1,0:T(4,128)} %bitcast.7, bf16[32,64,128]{2,1,0:T(8,128)(2,1)} %latent.5, bf16[128,64,128]{2,1,0:T(8,128)(2,1)} %pick.1.after), custom_call_target="tpu_custom_call" | custom-call | tf_op jit(solution)/shard_map/first_hop/pallas_call | solution.py:100
  15.4 0.1 collective-permute-start
  15.5 1.5 %collective-permute-done.passed = bf16[16,64,128]{2,1,0:T(8,128)(2,1)S(1)} collective-permute-done((bf16[16,64,128]{2,1,0:T(8,128)(2,1)S(1)}, bf16[16,64,128]{2,1,0:T(8,128)(2,1)S(1)}, u32[]{:S(2)}, u32[]{:S(2)}) %collective-permute-start) | collective-permute-done | bytes 262176 | tf_op jit(solution)/shard_map/ppermute | solution.py:171
  17.0 0.6 repack.2
  17.7 1.0 %collective-permute-start.1 = (bf16[8,64,128]{2,1,0:T(8,128)(2,1)S(1)}, bf16[8,64,128]{2,1,0:T(8,128)(2,1)S(1)}, u32[]{:S(2)}, u32[]{:S(2)}) collective-permute-start(bf16[8,64,128]{2,1,0:T(8,128)(2,1)S(1)} %get-tuple-element.20), channel_id=1, source_target_pairs={{0,2},{1,3},{2,0},{3,1},{4,6},{5,7},{6,4},{7,5},{8,10},{9,11},{10,... | collective-permute-start | bytes 393224 | tf_op jit(solution)/shard_map/ppermute | solution.py:177
  18.7 2.7 %collective-permute-start.2 = (bf16[8,64,128]{2,1,0:T(8,128)(2,1)S(1)}, bf16[8,64,128]{2,1,0:T(8,128)(2,1)S(1)}, u32[]{:S(2)}, u32[]{:S(2)}) collective-permute-start(bf16[8,64,128]{2,1,0:T(8,128)(2,1)S(1)} %get-tuple-element.21), channel_id=1, source_target_pairs={{0,4},{1,5},{2,6},{3,7},{4,0},{5,1},{6,2},{7,3},{8,12},{9,13},{10,... | collective-permute-start | bytes 393224 | tf_op jit(solution)/shard_map/ppermute | solution.py:177
  21.4 1.1 %collective-permute-start.3 = (bf16[8,64,128]{2,1,0:T(8,128)(2,1)S(1)}, bf16[8,64,128]{2,1,0:T(8,128)(2,1)S(1)}, u32[]{:S(2)}, u32[]{:S(2)}) collective-permute-start(bf16[8,64,128]{2,1,0:T(8,128)(2,1)S(1)} %get-tuple-element.22), channel_id=1, source_target_pairs={{0,6},{1,7},{2,4},{3,5},{4,2},{5,3},{6,0},{7,1},{8,14},{9,15},{10,... | collective-permute-start | bytes 393224 | tf_op jit(solution)/shard_map/ppermute | solution.py:177
  22.5 1.1 %collective-permute-start.4 = (bf16[8,64,128]{2,1,0:T(8,128)(2,1)S(1)}, bf16[8,64,128]{2,1,0:T(8,128)(2,1)S(1)}, u32[]{:S(2)}, u32[]{:S(2)}) collective-permute-start(bf16[8,64,128]{2,1,0:T(8,128)(2,1)S(1)} %get-tuple-element.23), channel_id=1, source_target_pairs={{0,8},{8,16},{16,24},{24,32},{32,40},{40,48},{48,56},{56,64},{64,7... | collective-permute-start | bytes 393224 | tf_op jit(solution)/shard_map/ppermute | solution.py:184
  23.5 4.3 %collective-permute-start.5 = (bf16[8,64,128]{2,1,0:T(8,128)(2,1)S(1)}, bf16[8,64,128]{2,1,0:T(8,128)(2,1)S(1)}, u32[]{:S(2)}, u32[]{:S(2)}) collective-permute-start(bf16[8,64,128]{2,1,0:T(8,128)(2,1)S(1)} %get-tuple-element.24), channel_id=1, source_target_pairs={{0,120},{8,0},{16,8},{24,16},{32,24},{40,32},{48,40},{56,48},{64,5... | collective-permute-start | bytes 393224 | tf_op jit(solution)/shard_map/ppermute | solution.py:184
  28.5 12.1 %collective-permute-done.1.rest_0_ = bf16[8,64,128]{2,1,0:T(8,128)(2,1)S(1)} collective-permute-done((bf16[8,64,128]{2,1,0:T(8,128)(2,1)S(1)}, bf16[8,64,128]{2,1,0:T(8,128)(2,1)S(1)}, u32[]{:S(2)}, u32[]{:S(2)}) %collective-permute-start.1) | collective-permute-done | bytes 131104 | tf_op jit(solution)/shard_map/ppermute | solution.py:177
  40.5 3.8 %collective-permute-done.2.rest_1_ = bf16[8,64,128]{2,1,0:T(8,128)(2,1)S(1)} collective-permute-done((bf16[8,64,128]{2,1,0:T(8,128)(2,1)S(1)}, bf16[8,64,128]{2,1,0:T(8,128)(2,1)S(1)}, u32[]{:S(2)}, u32[]{:S(2)}) %collective-permute-start.2) | collective-permute-done | bytes 131104 | tf_op jit(solution)/shard_map/ppermute | solution.py:177
  44.5 5.1 %first_step.1 = (bf16[80,64,128]{2,1,0:T(8,128)(2,1)S(1)}, bf16[16,64,128]{2,1,0:T(8,128)(2,1)S(1)}, bf16[2048,128]{1,0:T(8,128)(2,1)S(1)}, bf16[32,64,1024]{2,1,0:T(8,128)(2,1)S(1)}) custom-call(s32[1]{0:T(128)S(6)} %copy.17.count, s32[16,32]{1,0:T(8,128)} %bitcast.12, s32[4,8]{1,0:T(4,128)} %bitcast.8, s32[4,32]{1,0:T(4,128)} %bitcast.16, ...), custom_call_target="tpu_custom_call" | custom-call | tf_op jit(solution)/shard_map/first_step/pallas_call | solution.py:327
  49.7 1.5 %collective-permute-done.6.passed = bf16[16,64,128]{2,1,0:T(8,128)(2,1)S(1)} collective-permute-done((bf16[16,64,128]{2,1,0:T(8,128)(2,1)S(1)}, bf16[16,64,128]{2,1,0:T(8,128)(2,1)S(1)}, u32[]{:S(2)}, u32[]{:S(2)}) %collective-permute-start.6) | collective-permute-done | bytes 262176 | tf_op jit(solution)/shard_map/ppermute | solution.py:171
  51.3 0.6 repack.3
  51.9 1.4 %collective-permute-start.7 = (bf16[8,64,128]{2,1,0:T(8,128)(2,1)S(1)}, bf16[8,64,128]{2,1,0:T(8,128)(2,1)S(1)}, u32[]{:S(2)}, u32[]{:S(2)}) collective-permute-start(bf16[8,64,128]{2,1,0:T(8,128)(2,1)S(1)} %get-tuple-element.29), channel_id=1, source_target_pairs={{0,2},{1,3},{2,0},{3,1},{4,6},{5,7},{6,4},{7,5},{8,10},{9,11},{10,... | collective-permute-start | bytes 393224 | tf_op jit(solution)/shard_map/ppermute | solution.py:177
  53.3 2.7 %collective-permute-start.8 = (bf16[8,64,128]{2,1,0:T(8,128)(2,1)S(1)}, bf16[8,64,128]{2,1,0:T(8,128)(2,1)S(1)}, u32[]{:S(2)}, u32[]{:S(2)}) collective-permute-start(bf16[8,64,128]{2,1,0:T(8,128)(2,1)S(1)} %get-tuple-element.30), channel_id=1, source_target_pairs={{0,4},{1,5},{2,6},{3,7},{4,0},{5,1},{6,2},{7,3},{8,12},{9,13},{10,... | collective-permute-start | bytes 393224 | tf_op jit(solution)/shard_map/ppermute | solution.py:177
  56.0 0.7 collective-permute-start.9
  56.7 1.6 %collective-permute-start.10 = (bf16[8,64,128]{2,1,0:T(8,128)(2,1)S(1)}, bf16[8,64,128]{2,1,0:T(8,128)(2,1)S(1)}, u32[]{:S(2)}, u32[]{:S(2)}) collective-permute-start(bf16[8,64,128]{2,1,0:T(8,128)(2,1)S(1)} %get-tuple-element.32), channel_id=1, source_target_pairs={{0,8},{8,16},{16,24},{24,32},{32,40},{40,48},{48,56},{56,64},{64,7... | collective-permute-start | bytes 393224 | tf_op jit(solution)/shard_map/ppermute | solution.py:184
  58.3 4.1 %collective-permute-start.11 = (bf16[8,64,128]{2,1,0:T(8,128)(2,1)S(1)}, bf16[8,64,128]{2,1,0:T(8,128)(2,1)S(1)}, u32[]{:S(2)}, u32[]{:S(2)}) collective-permute-start(bf16[8,64,128]{2,1,0:T(8,128)(2,1)S(1)} %get-tuple-element.33), channel_id=1, source_target_pairs={{0,120},{8,0},{16,8},{24,16},{32,24},{40,32},{48,40},{56,48},{64,5... | collective-permute-start | bytes 393224 | tf_op jit(solution)/shard_map/ppermute | solution.py:184
  62.4 2.2 %collective-permute-done.9.rest_2_ = bf16[8,64,128]{2,1,0:T(8,128)(2,1)S(1)} collective-permute-done((bf16[8,64,128]{2,1,0:T(8,128)(2,1)S(1)}, bf16[8,64,128]{2,1,0:T(8,128)(2,1)S(1)}, u32[]{:S(2)}, u32[]{:S(2)}) %collective-permute-start.9) | collective-permute-done | bytes 131104 | tf_op jit(solution)/shard_map/ppermute | solution.py:177
  64.7 0.6 collective-permute-done.10.rest_3_
  65.4 3.9 %second_step.1 = (bf16[80,64,128]{2,1,0:T(8,128)(2,1)S(1)}, bf16[32,64,128]{2,1,0:T(8,128)(2,1)}) custom-call(s32[16,32]{1,0:T(8,128)S(1)} %bitcast.13, s32[1]{0:T(128)S(6)} %copy.17.count, bf16[32,64,1024]{2,1,0:T(8,128)(2,1)S(1)} %get-tuple-element.25.weights, bf16[2048,128]{1,0:T(8,128)(2,1)S(1)} %get-tuple-element.26.interp, ...), custom_call_target="tpu_custom_call", output_to_operand_aliasing={{0}: (8, {})} | custom-call | tf_op jit(solution)/shard_map/second_step/pallas_call | solution.py:385
  (26 shorter events, 0.2 us)
Async XLA Ops:
  2.3 42.1 %all-to-all-start = ((bf16[128,64,128]{2,1,0:T(8,128)(2,1)}), bf16[128,64,128]{2,1,0:T(8,128)(2,1)S(1)}, u32[]{:S(2)}, u32[]{:S(2)}) async-start(bf16[128,64,128]{2,1,0:T(8,128)(2,1)} %pick.1.after), calls=%async_computation | async-start | bytes 4194304 | tf_op jit(solution)/shard_map/all_to_all | solution.py:421
  13.5 3.5 %copy-start = (bf16[32,64,128]{2,1,0:T(8,128)(2,1)S(1)}, bf16[32,64,128]{2,1,0:T(8,128)(2,1)}, u32[]{:S(2)}) copy-start(bf16[32,64,128]{2,1,0:T(8,128)(2,1)} %latent.5) | copy-start | bytes 1572868
  13.5 3.5 %copy-start.3 = (s32[1,8,4]{1,2,0:T(4,128)S(1)}, s32[1,8,4]{1,2,0:T(4,128)}, u32[]{:S(2)}) copy-start(s32[1,8,4]{1,2,0:T(4,128)} %param.21) | copy-start | bytes 388
  13.5 3.5 %copy-start.8 = (s32[1,2,8]{2,1,0:T(2,128)S(1)}, s32[1,2,8]{2,1,0:T(2,128)}, u32[]{:S(2)}) copy-start(s32[1,2,8]{2,1,0:T(2,128)} %param.22) | copy-start | bytes 196
  15.4 1.6 %collective-permute-start = (bf16[16,64,128]{2,1,0:T(8,128)(2,1)S(1)}, bf16[16,64,128]{2,1,0:T(8,128)(2,1)S(1)}, u32[]{:S(2)}, u32[]{:S(2)}) collective-permute-start(bf16[16,64,128]{2,1,0:T(8,128)(2,1)S(1)} %first_hop.1), channel_id=1, source_target_pairs={{0,1},{1,0},{2,3},{3,2},{4,5},{5,4},{6,7},{7,6},{8,9},{9,8},{10,11... | collective-permute-start | bytes 786440 | tf_op jit(solution)/shard_map/ppermute | solution.py:171
  17.7 22.9 %collective-permute-start.1 = (bf16[8,64,128]{2,1,0:T(8,128)(2,1)S(1)}, bf16[8,64,128]{2,1,0:T(8,128)(2,1)S(1)}, u32[]{:S(2)}, u32[]{:S(2)}) collective-permute-start(bf16[8,64,128]{2,1,0:T(8,128)(2,1)S(1)} %get-tuple-element.20), channel_id=1, source_target_pairs={{0,2},{1,3},{2,0},{3,1},{4,6},{5,7},{6,4},{7,5},{8,10},{9,11},{10,... | collective-permute-start | bytes 393224 | tf_op jit(solution)/shard_map/ppermute | solution.py:177
  18.7 25.7 %collective-permute-start.2 = (bf16[8,64,128]{2,1,0:T(8,128)(2,1)S(1)}, bf16[8,64,128]{2,1,0:T(8,128)(2,1)S(1)}, u32[]{:S(2)}, u32[]{:S(2)}) collective-permute-start(bf16[8,64,128]{2,1,0:T(8,128)(2,1)S(1)} %get-tuple-element.21), channel_id=1, source_target_pairs={{0,4},{1,5},{2,6},{3,7},{4,0},{5,1},{6,2},{7,3},{8,12},{9,13},{10,... | collective-permute-start | bytes 393224 | tf_op jit(solution)/shard_map/ppermute | solution.py:177
  21.4 23.0 %collective-permute-start.3 = (bf16[8,64,128]{2,1,0:T(8,128)(2,1)S(1)}, bf16[8,64,128]{2,1,0:T(8,128)(2,1)S(1)}, u32[]{:S(2)}, u32[]{:S(2)}) collective-permute-start(bf16[8,64,128]{2,1,0:T(8,128)(2,1)S(1)} %get-tuple-element.22), channel_id=1, source_target_pairs={{0,6},{1,7},{2,4},{3,5},{4,2},{5,3},{6,0},{7,1},{8,14},{9,15},{10,... | collective-permute-start | bytes 393224 | tf_op jit(solution)/shard_map/ppermute | solution.py:177
  22.5 21.9 %collective-permute-start.4 = (bf16[8,64,128]{2,1,0:T(8,128)(2,1)S(1)}, bf16[8,64,128]{2,1,0:T(8,128)(2,1)S(1)}, u32[]{:S(2)}, u32[]{:S(2)}) collective-permute-start(bf16[8,64,128]{2,1,0:T(8,128)(2,1)S(1)} %get-tuple-element.23), channel_id=1, source_target_pairs={{0,8},{8,16},{16,24},{24,32},{32,40},{40,48},{48,56},{56,64},{64,7... | collective-permute-start | bytes 393224 | tf_op jit(solution)/shard_map/ppermute | solution.py:184
  23.5 20.9 %collective-permute-start.5 = (bf16[8,64,128]{2,1,0:T(8,128)(2,1)S(1)}, bf16[8,64,128]{2,1,0:T(8,128)(2,1)S(1)}, u32[]{:S(2)}, u32[]{:S(2)}) collective-permute-start(bf16[8,64,128]{2,1,0:T(8,128)(2,1)S(1)} %get-tuple-element.24), channel_id=1, source_target_pairs={{0,120},{8,0},{16,8},{24,16},{32,24},{40,32},{48,40},{56,48},{64,5... | collective-permute-start | bytes 393224 | tf_op jit(solution)/shard_map/ppermute | solution.py:184
  44.4 6.8 %copy-start.4 = (s32[1,8,4]{1,2,0:T(4,128)S(1)}, s32[1,8,4]{1,2,0:T(4,128)}, u32[]{:S(2)}) copy-start(s32[1,8,4]{1,2,0:T(4,128)} %param.21) | copy-start | bytes 388
  44.4 20.9 %copy-start.1 = (bf16[2,384,128]{2,1,0:T(8,128)(2,1)S(1)}, bf16[2,384,128]{2,1,0:T(8,128)(2,1)}, u32[]{:S(2)}) copy-start(bf16[2,384,128]{2,1,0:T(8,128)(2,1)} %w_in.3) | copy-start | bytes 589828
  44.4 20.9 %copy-start.2 = (bf16[2,128,128]{2,1,0:T(8,128)(2,1)S(1)}, bf16[2,128,128]{2,1,0:T(8,128)(2,1)}, u32[]{:S(2)}) copy-start(bf16[2,128,128]{2,1,0:T(8,128)(2,1)} %w_out.3) | copy-start | bytes 196612
  44.5 20.9 %copy-start.5 = (s32[32,16]{0,1:T(8,128)S(1)}, s32[32,16]{0,1:T(8,128)}, u32[]{:S(2)}) copy-start(s32[32,16]{0,1:T(8,128)} %param.16) | copy-start | bytes 6148
  44.5 20.9 %copy-start.6 = (f32[2,128]{1,0:T(2,128)S(1)}, f32[2,128]{1,0:T(2,128)}, u32[]{:S(2)}) copy-start(f32[2,128]{1,0:T(2,128)} %b_in.3) | copy-start | bytes 3076
  44.5 20.9 %copy-start.7 = (f32[2,128]{1,0:T(2,128)S(1)}, f32[2,128]{1,0:T(2,128)}, u32[]{:S(2)}) copy-start(f32[2,128]{1,0:T(2,128)} %gain.3) | copy-start | bytes 3076
  49.6 1.6 %collective-permute-start.6 = (bf16[16,64,128]{2,1,0:T(8,128)(2,1)S(1)}, bf16[16,64,128]{2,1,0:T(8,128)(2,1)S(1)}, u32[]{:S(2)}, u32[]{:S(2)}) collective-permute-start(bf16[16,64,128]{2,1,0:T(8,128)(2,1)S(1)} %get-tuple-element.28), channel_id=1, source_target_pairs={{0,1},{1,0},{2,3},{3,2},{4,5},{5,4},{6,7},{7,6},{8,9},{9,8},{10,11... | collective-permute-start | bytes 786440 | tf_op jit(solution)/shard_map/ppermute | solution.py:171
  51.9 10.5 %collective-permute-start.7 = (bf16[8,64,128]{2,1,0:T(8,128)(2,1)S(1)}, bf16[8,64,128]{2,1,0:T(8,128)(2,1)S(1)}, u32[]{:S(2)}, u32[]{:S(2)}) collective-permute-start(bf16[8,64,128]{2,1,0:T(8,128)(2,1)S(1)} %get-tuple-element.29), channel_id=1, source_target_pairs={{0,2},{1,3},{2,0},{3,1},{4,6},{5,7},{6,4},{7,5},{8,10},{9,11},{10,... | collective-permute-start | bytes 393224 | tf_op jit(solution)/shard_map/ppermute | solution.py:177
  53.3 9.2 %collective-permute-start.8 = (bf16[8,64,128]{2,1,0:T(8,128)(2,1)S(1)}, bf16[8,64,128]{2,1,0:T(8,128)(2,1)S(1)}, u32[]{:S(2)}, u32[]{:S(2)}) collective-permute-start(bf16[8,64,128]{2,1,0:T(8,128)(2,1)S(1)} %get-tuple-element.30), channel_id=1, source_target_pairs={{0,4},{1,5},{2,6},{3,7},{4,0},{5,1},{6,2},{7,3},{8,12},{9,13},{10,... | collective-permute-start | bytes 393224 | tf_op jit(solution)/shard_map/ppermute | solution.py:177
  56.0 8.7 %collective-permute-start.9 = (bf16[8,64,128]{2,1,0:T(8,128)(2,1)S(1)}, bf16[8,64,128]{2,1,0:T(8,128)(2,1)S(1)}, u32[]{:S(2)}, u32[]{:S(2)}) collective-permute-start(bf16[8,64,128]{2,1,0:T(8,128)(2,1)S(1)} %get-tuple-element.31), channel_id=1, source_target_pairs={{0,6},{1,7},{2,4},{3,5},{4,2},{5,3},{6,0},{7,1},{8,14},{9,15},{10,... | collective-permute-start | bytes 393224 | tf_op jit(solution)/shard_map/ppermute | solution.py:177
  56.7 8.6 %collective-permute-start.10 = (bf16[8,64,128]{2,1,0:T(8,128)(2,1)S(1)}, bf16[8,64,128]{2,1,0:T(8,128)(2,1)S(1)}, u32[]{:S(2)}, u32[]{:S(2)}) collective-permute-start(bf16[8,64,128]{2,1,0:T(8,128)(2,1)S(1)} %get-tuple-element.32), channel_id=1, source_target_pairs={{0,8},{8,16},{16,24},{24,32},{32,40},{40,48},{48,56},{56,64},{64,7... | collective-permute-start | bytes 393224 | tf_op jit(solution)/shard_map/ppermute | solution.py:184
  58.3 7.0 %collective-permute-start.11 = (bf16[8,64,128]{2,1,0:T(8,128)(2,1)S(1)}, bf16[8,64,128]{2,1,0:T(8,128)(2,1)S(1)}, u32[]{:S(2)}, u32[]{:S(2)}) collective-permute-start(bf16[8,64,128]{2,1,0:T(8,128)(2,1)S(1)} %get-tuple-element.33), channel_id=1, source_target_pairs={{0,120},{8,0},{16,8},{24,16},{32,24},{40,32},{48,40},{56,48},{64,5... | collective-permute-start | bytes 393224 | tf_op jit(solution)/shard_map/ppermute | solution.py:184

commit v2 on v1

--- a/solution.py
+++ b/solution.py
@@ -13,7 +13,6 @@
 VMEM = pl.BlockSpec(memory_space=pltpu.VMEM)
 ANY = pl.BlockSpec(memory_space=pl.ANY)
 CORES = 2
-AHEAD = 2
 
 
 def in_hbm(array):
@@ -260,53 +259,71 @@
     return first + lax.broadcasted_iota(jnp.int32, (size, 1), 0) < count
 
 
-def first_kernel(
-    count, ids, sub_ids, slots, received, weights, interp_weights, w_in, b_in, w_out, gain, latent,
-    passed, *rest,
+def prepare_kernel(
+    slots, received, weights, interp_weights, w_in, b_in, w_out, gain, latent,
+    interp, held, pool, *rest,
 ):
-    ways = sub_ids.shape[1] // CORES - 1
-    pieces, (below, above, *rest) = rest[:ways], rest[ways:]
-    pool, other, interp, held, summed, coarse, *rest = rest
-    tables, net, sems = rest[:3], rest[3:7], rest[7:]
-    table_sems, interp_sems, own_sem, in_sems, network_sems = sems
-    tabling = [
-        pltpu.make_async_copy(source, target, table_sems.at[position])
-        for position, (source, target) in enumerate(zip((slots, sub_ids, ids), tables))
+    net, (slots_held, coarse, slots_sem, interp_sems, own_sem, in_sem, network_sems) = rest[:4], rest[4:]
+    table = pltpu.make_async_copy(slots, slots_held, slots_sem)
+    table.start()
+    arriving = chunked(interp_weights, coarse, interp_sems)
+    start(arriving)
+    blocks = latent.shape[0]
+    more = [
+        pltpu.make_async_copy(latent, pool.at[pl.ds(0, blocks)], own_sem),
+        pltpu.make_async_copy(weights, held, in_sem),
     ]
-    start(tabling)
-    slots, sub_ids, ids = tables
-    coarse_arriving = chunked(interp_weights, coarse, interp_sems)
-    arriving = chunked(weights, held, in_sems)
-    blocks, rows, lat = latent.shape
-    bring = pltpu.make_async_copy(latent, pool.at[pl.ds(0, blocks)], own_sem)
-    network = [
+    more += [
         pltpu.make_async_copy(source, target, network_sems.at[position])
         for position, (source, target) in enumerate(zip((w_in, b_in, w_out, gain), net))
     ]
-    start(coarse_arriving)
-    bring.start()
-    queue = arriving + network
-    start(queue[:AHEAD])
-    queue = queue[AHEAD:]
-    w_in, b_in, w_out, gain = net
-    wait(tabling)
-    fill_pool(pool, blocks, sub_ids, passed, pieces, below, above)
-    size = blocks // len(coarse_arriving)
-    for part, copy in enumerate(coarse_arriving):
-        copy.wait()
-        start(queue[:1])
-        queue = queue[1:]
-        products(coarse, received, slots, interp, part * size, (part + 1) * size)
-    bring.wait()
-    copy_to_self(pool, sub_ids, blocks)
+    table.wait()
     size = blocks // len(arriving)
     for part, copy in enumerate(arriving):
         copy.wait()
-        start(queue[:2])
-        queue = queue[2:]
-        products(held, pool, ids, summed, part * size, (part + 1) * size)
-    start(queue)
-    wait(network)
+        if part == 0:
+            start(more)
+        products(coarse, received, slots_held, interp, part * size, (part + 1) * size)
+    wait(more)
+
+
+def prepare(received, slots, interp_weights, latent, pool, weights, network):
+    blocks, rows, lat = latent.shape
+    return pl.pallas_call(
+        prepare_kernel,
+        in_specs=[ANY, VMEM] + [ANY] * 7,
+        out_specs=[VMEM] * 7,
+        out_shape=[
+            jax.ShapeDtypeStruct((blocks * rows, lat), BF16),
+            pltpu.VMEM(weights.shape, BF16),
+            pltpu.VMEM((pool, rows, lat), BF16),
+            *(pltpu.VMEM(part.shape, part.dtype) for part in network),
+        ],
+        scratch_shapes=[
+            pltpu.SMEM(slots.shape, jnp.int32),
+            pltpu.VMEM(interp_weights.shape, BF16),
+            pltpu.SemaphoreType.DMA,
+            pltpu.SemaphoreType.DMA((2,)),
+            pltpu.SemaphoreType.DMA,
+            pltpu.SemaphoreType.DMA,
+            pltpu.SemaphoreType.DMA((4,)),
+        ],
+        compiler_params=params(8),
+        name="prepare",
+    )(in_hbm(slots), received, *map(in_hbm, (weights, interp_weights, *network, latent)))
+
+
+def first_kernel(
+    count, ids, sub_ids, weights, interp, w_in, b_in, w_out, gain, pool_in, passed, *rest
+):
+    del pool_in
+    ways = sub_ids.shape[1] // CORES - 1
+    pieces, (below, above, pool, other, summed) = rest[:ways], rest[ways:]
+    blocks = weights.shape[0]
+    rows, lat = pool.shape[1:]
+    fill_pool(pool, blocks, sub_ids, passed, pieces, below, above)
+    copy_to_self(pool, sub_ids, blocks)
+    products(weights, pool, ids, summed, 0, blocks)
     own = pool[pl.ds(0, blocks)].reshape(blocks * rows, lat)
     joined = jnp.concatenate([own, summed[...], interp[...]], axis=1)
     hidden = jnp.dot(joined, w_in[0], preferred_element_type=F32) + b_in[0:1]
@@ -317,40 +334,23 @@
     copy_to_self(pool, sub_ids, blocks)
 
 
-def first_step(
-    received, slots, interp_weights, latent, halo, ids, weights, w_in, b_in, w_out, gain, count,
-    sub_ids,
-):
-    blocks, rows, lat = latent.shape
-    pool = blocks + sub_ids.size + 2 * halo[-1].shape[0]
-    network = (w_in, b_in, w_out, gain)
+def first_step(pool, halo, weights, interp, ids, network, count, sub_ids):
+    rows, lat = pool.shape[1:]
+    blocks = weights.shape[0]
+    operands = [count, ids, sub_ids, *map(in_vmem, (weights, interp, *network, pool))]
     return pl.pallas_call(
         first_kernel,
-        in_specs=[SMEM, ANY, ANY, ANY, VMEM] + [ANY] * 7 + [VMEM] * len(halo),
-        out_specs=[VMEM] * 4,
+        in_specs=[SMEM] * 3 + [VMEM] * (7 + len(halo)),
+        out_specs=[VMEM] * 2,
         out_shape=[
-            pltpu.VMEM((pool, rows, lat), BF16),
-            blocks_like(sub_ids.size // CORES, latent),
-            jax.ShapeDtypeStruct((blocks * rows, lat), BF16),
-            pltpu.VMEM(weights.shape, BF16),
+            pltpu.VMEM(pool.shape, BF16),
+            jax.ShapeDtypeStruct((sub_ids.size // CORES, rows, lat), BF16),
         ],
-        scratch_shapes=[
-            pltpu.VMEM((blocks * rows, lat), BF16),
-            pltpu.VMEM(interp_weights.shape, BF16),
-            *(pltpu.SMEM(part.shape, jnp.int32) for part in (slots, sub_ids, ids)),
-            *(pltpu.VMEM(part.shape, part.dtype) for part in network),
-            pltpu.SemaphoreType.DMA((3,)),
-            pltpu.SemaphoreType.DMA((2,)),
-            pltpu.SemaphoreType.DMA,
-            pltpu.SemaphoreType.DMA((4,)),
-            pltpu.SemaphoreType.DMA((4,)),
-        ],
+        input_output_aliases={len(operands) - 1: 0},
+        scratch_shapes=[pltpu.VMEM((blocks * rows, lat), BF16)],
         compiler_params=params(16),
         name="first_step",
-    )(
-        count, *map(in_hbm, (ids, sub_ids, slots)), received,
-        *map(in_hbm, (weights, interp_weights, *network, latent)), *halo,
-    )
+    )(*operands, *halo)
 
 
 def second_kernel(
@@ -378,10 +378,10 @@
     wait(copies)
 
 
-def second_step(pool, halo, weights, interp, ids, w_in, b_in, w_out, gain, count, sub_ids):
+def second_step(pool, halo, weights, interp, ids, network, count, sub_ids):
     rows, lat = pool.shape[1:]
     blocks = weights.shape[0]
-    operands = [ids, count, in_vmem(weights), interp, w_in, b_in, w_out, gain, in_vmem(pool)]
+    operands = [ids, count, *map(in_vmem, (weights, interp, *network, pool))]
     return pl.pallas_call(
         second_kernel,
         in_specs=[SMEM] * 2 + [VMEM] * 7 + [ANY] + [VMEM] * len(halo),
@@ -420,14 +420,14 @@
     payload = pick(coarse_latent, coarse_send.reshape(1, -1))
     received = lax.all_to_all(payload, ("dom", "sub"), split_axis=0, concat_axis=0, tiled=True)
     halo = second_hop(fine_latent, first_hop(fine_latent, sub_ids, payload), sub_ids, dom_ids)
-    pool, other, interp, weights = first_step(
-        received, interp_slot.T, interp_weight, fine_latent, halo, adj_ids, adj_weight, w_in, b_in,
-        w_out, ln_gain, block_count, sub_ids,
+    size = fine_latent.shape[0] + sub_ids.size + dom_ids.size
+    interp, weights, pool, *network = prepare(
+        received, interp_slot.T, interp_weight, fine_latent, size, adj_weight,
+        (w_in, b_in, w_out, ln_gain),
     )
+    pool, other = first_step(pool, halo, weights, interp, adj_ids, network, block_count, sub_ids)
     halo = second_hop(pool, other, sub_ids, dom_ids)
-    return second_step(
-        pool, halo, weights, interp, adj_ids, w_in, b_in, w_out, ln_gain, block_count, sub_ids
-    )
+    return second_step(pool, halo, weights, interp, adj_ids, network, block_count, sub_ids)
 
 
 def solution(mesh):

time: 69.7 us -> 73.8 us (1.059)
  Pallas kernels: 14.5 us -> 17.1 us
  waiting for transfers between devices: 21.9 us -> 23.6 us
    all_to_all x1, waiting for transfers between devices: 0.01 us -> 15.3 us  [per_device(): lax.all_to_all(payload, ('dom', 'sub'), split_axis=0, concat_axis=0, tile...]
    ppermute x6, waiting for transfers between devices: 18.3 us -> 5.24 us  [along_x(): lax.ppermute(piece, 'sub', [(i, i ^ way * CORES) for i in range(size)])]
    pallas_call x1 -> x2, Pallas kernels: 5.14 us -> 7.06 us  [the longest x1 3.76 us: prepare(): pl.pallas_call(prepare_kernel, in_specs=[ANY, VMEM] + [ANY] * 7, out_spec...]
  transfers between devices with their start and end apart: 13 -> 13, of which waited for: 7 -> 6; matrix products, arithmetic and copies ran while one was open for 0% -> 0% of each run, Pallas kernels for 4% -> 10%
where the time goes in v2:
time: 73.8 us; the launch traced here: 73 us
  starting transfers between devices  31.5 us (43%)
  waiting for transfers between devices  23.6 us (32%)
  Pallas kernels  17.1 us (23%)
  between operations  0.8 us (1%)
    all_to_all x1, waiting for transfers between devices, per_device(): lax.all_to_all(payload, ('dom', 'sub'), split_axis=0, concat_axis=0, tile...  15.3 us
    all_to_all x1, starting transfers between devices, per_device(): lax.all_to_all(payload, ('dom', 'sub'), split_axis=0, concat_axis=0, tile...  11.1 us
    ppermute x4, starting transfers between devices, along_dom(): lax.ppermute(blocks, 'dom', [(i, (i + distance) % size) for i in range(si...  10.8 us
    ppermute x6, starting transfers between devices, along_x(): lax.ppermute(piece, 'sub', [(i, i ^ way * CORES) for i in range(size)])  9.4 us
    ppermute x6, waiting for transfers between devices, along_x(): lax.ppermute(piece, 'sub', [(i, i ^ way * CORES) for i in range(size)])  5.24 us
    pallas_call x1, Pallas kernels, second_step(): pl.pallas_call(second_kernel, in_specs=[SMEM] * 2 + [VMEM] * 7 + [ANY] +...  3.91 us
    pallas_call x1, Pallas kernels, prepare(): pl.pallas_call(prepare_kernel, in_specs=[ANY, VMEM] + [ANY] * 7, out_spec...  3.76 us
    pallas_call x1, Pallas kernels, first_step(): pl.pallas_call(first_kernel, in_specs=[SMEM] * 3 + [VMEM] * (7 + len(halo...  3.3 us
  transfers between devices with their start and end apart: 13, of which 6 were waited for; matrix products, arithmetic and copies ran while one was open for 0% of the time, Pallas kernels for 10%

profile of v2, /device:TPU:0, one launch (start us, length us, event | category | flops | bytes accessed | tf_op | source)
XLA Modules:
  0.0 73.0 jit_solution(16539457636200574358)
XLA Ops:
  0.0 2.3 %pick.1.after = bf16[128,64,128]{2,1,0:T(8,128)(2,1)} custom-call(s32[1,128]{1,0:T(1,128)} %bitcast.17, bf16[8,64,128]{2,1,0:T(8,128)(2,1)} %table.1), custom_call_target="tpu_custom_call" | custom-call | tf_op jit(solution)/shard_map/pick/pallas_call | solution.py:133
  2.3 11.1 %all-to-all-start = ((bf16[128,64,128]{2,1,0:T(8,128)(2,1)}), bf16[128,64,128]{2,1,0:T(8,128)(2,1)S(1)}, u32[]{:S(2)}, u32[]{:S(2)}) async-start(bf16[128,64,128]{2,1,0:T(8,128)(2,1)} %pick.1.after), calls=%async_computation | async-start | bytes 4194304 | tf_op jit(solution)/shard_map/all_to_all | solution.py:421
  13.5 1.9 %first_hop.1 = bf16[16,64,128]{2,1,0:T(8,128)(2,1)S(1)} custom-call(s32[4,8]{1,0:T(4,128)} %bitcast.7, bf16[32,64,128]{2,1,0:T(8,128)(2,1)} %latent.5, bf16[128,64,128]{2,1,0:T(8,128)(2,1)} %pick.1.after), custom_call_target="tpu_custom_call" | custom-call | tf_op jit(solution)/shard_map/first_hop/pallas_call | solution.py:99
  15.5 1.5 %collective-permute-done.passed = bf16[16,64,128]{2,1,0:T(8,128)(2,1)S(1)} collective-permute-done((bf16[16,64,128]{2,1,0:T(8,128)(2,1)S(1)}, bf16[16,64,128]{2,1,0:T(8,128)(2,1)S(1)}, u32[]{:S(2)}, u32[]{:S(2)}) %collective-permute-start) | collective-permute-done | bytes 262176 | tf_op jit(solution)/shard_map/ppermute | solution.py:170
  17.1 1.3 %repack.2 = (bf16[8,64,128]{2,1,0:T(8,128)(2,1)}, bf16[8,64,128]{2,1,0:T(8,128)(2,1)S(1)}, bf16[8,64,128]{2,1,0:T(8,128)(2,1)S(1)}, bf16[8,64,128]{2,1,0:T(8,128)(2,1)S(1)}, bf16[8,64,128]{2,1,0:T(8,128)(2,1)S(1)}) custom-call(s32[4,8]{1,0:T(4,128)S(1)} %bitcast.8, s32[2,8]{1,0:T(2,128)S(1)} %bitcast.14, bf16[32,64,128]{2,1,0:T(8,128)(2,1)S(1)} %copy-done, ...), custom_call_target="tpu_custom_call" | custom-call | tf_op jit(solution)/shard_map/repack/pallas_call | solution.py:159
  18.4 0.9 %collective-permute-start.1 = (bf16[8,64,128]{2,1,0:T(8,128)(2,1)}, bf16[8,64,128]{2,1,0:T(8,128)(2,1)S(1)}, u32[]{:S(2)}, u32[]{:S(2)}) collective-permute-start(bf16[8,64,128]{2,1,0:T(8,128)(2,1)} %get-tuple-element.32), channel_id=1, source_target_pairs={{0,2},{1,3},{2,0},{3,1},{4,6},{5,7},{6,4},{7,5},{8,10},{9,11},{10,... | collective-permute-start | bytes 393224 | tf_op jit(solution)/shard_map/ppermute | solution.py:176
  19.3 2.7 %collective-permute-start.2 = (bf16[8,64,128]{2,1,0:T(8,128)(2,1)S(1)}, bf16[8,64,128]{2,1,0:T(8,128)(2,1)S(1)}, u32[]{:S(2)}, u32[]{:S(2)}) collective-permute-start(bf16[8,64,128]{2,1,0:T(8,128)(2,1)S(1)} %get-tuple-element.33), channel_id=1, source_target_pairs={{0,4},{1,5},{2,6},{3,7},{4,0},{5,1},{6,2},{7,3},{8,12},{9,13},{10,... | collective-permute-start | bytes 393224 | tf_op jit(solution)/shard_map/ppermute | solution.py:176
  22.0 1.1 %collective-permute-start.3 = (bf16[8,64,128]{2,1,0:T(8,128)(2,1)S(1)}, bf16[8,64,128]{2,1,0:T(8,128)(2,1)S(1)}, u32[]{:S(2)}, u32[]{:S(2)}) collective-permute-start(bf16[8,64,128]{2,1,0:T(8,128)(2,1)S(1)} %get-tuple-element.34), channel_id=1, source_target_pairs={{0,6},{1,7},{2,4},{3,5},{4,2},{5,3},{6,0},{7,1},{8,14},{9,15},{10,... | collective-permute-start | bytes 393224 | tf_op jit(solution)/shard_map/ppermute | solution.py:176
  23.1 1.1 %collective-permute-start.4 = (bf16[8,64,128]{2,1,0:T(8,128)(2,1)S(1)}, bf16[8,64,128]{2,1,0:T(8,128)(2,1)S(1)}, u32[]{:S(2)}, u32[]{:S(2)}) collective-permute-start(bf16[8,64,128]{2,1,0:T(8,128)(2,1)S(1)} %get-tuple-element.35), channel_id=1, source_target_pairs={{0,8},{8,16},{16,24},{24,32},{32,40},{40,48},{48,56},{56,64},{64,7... | collective-permute-start | bytes 393224 | tf_op jit(solution)/shard_map/ppermute | solution.py:183
  24.1 4.3 %collective-permute-start.5 = (bf16[8,64,128]{2,1,0:T(8,128)(2,1)S(1)}, bf16[8,64,128]{2,1,0:T(8,128)(2,1)S(1)}, u32[]{:S(2)}, u32[]{:S(2)}) collective-permute-start(bf16[8,64,128]{2,1,0:T(8,128)(2,1)S(1)} %get-tuple-element.36), channel_id=1, source_target_pairs={{0,120},{8,0},{16,8},{24,16},{32,24},{40,32},{48,40},{56,48},{64,5... | collective-permute-start | bytes 393224 | tf_op jit(solution)/shard_map/ppermute | solution.py:183
  29.1 15.3 %all-to-all-done.received = bf16[128,64,128]{2,1,0:T(8,128)(2,1)S(1)} async-done(((bf16[128,64,128]{2,1,0:T(8,128)(2,1)}), bf16[128,64,128]{2,1,0:T(8,128)(2,1)S(1)}, u32[]{:S(2)}, u32[]{:S(2)}) %all-to-all-start) | async-done | bytes 2097184 | tf_op jit(solution)/shard_map/all_to_all | solution.py:421
  44.4 3.8 %prepare.1 = (bf16[2048,128]{1,0:T(8,128)(2,1)S(1)}, bf16[32,64,1024]{2,1,0:T(8,128)(2,1)S(1)}, bf16[80,64,128]{2,1,0:T(8,128)(2,1)S(1)}, bf16[2,384,128]{2,1,0:...) custom-call(s32[4,32]{1,0:T(4,128)} %bitcast.16, ...), custom_call_target="tpu_custom_call" | custom-call | tf_op jit(solution)/shard_map/prepare/pallas_call | solution.py:292
  48.2 3.3 %first_step.1 = (bf16[80,64,128]{2,1,0:T(8,128)(2,1)S(1)}, bf16[16,64,128]{2,1,0:T(8,128)(2,1)S(1)}) custom-call(s32[1]{0:T(128)S(6)} %copy.19.count, s32[16,32]{1,0:T(8,128)S(1)} %bitcast.12, s32[4,8]{1,0:T(4,128)S(1)} %bitcast.9, bf16[32,64,1024]{2,1,0:T(8,128)(2,1)S(1)} %get-tuple-element.25.weights, ...), custom_call_target="tpu_custom_call", output_to_operand_aliasing={{0}: (9, {})} | custom-call | tf_op jit(solution)/shard_map/first_step/pallas_call | solution.py:341
  51.6 1.5 %collective-permute-done.6.passed = bf16[16,64,128]{2,1,0:T(8,128)(2,1)S(1)} collective-permute-done((bf16[16,64,128]{2,1,0:T(8,128)(2,1)S(1)}, bf16[16,64,128]{2,1,0:T(8,128)(2,1)S(1)}, u32[]{:S(2)}, u32[]{:S(2)}) %collective-permute-start.6) | collective-permute-done | bytes 262176 | tf_op jit(solution)/shard_map/ppermute | solution.py:170
  53.1 0.6 repack.3
  53.8 0.7 collective-permute-start.10
  54.4 4.7 %collective-permute-start.11 = (bf16[8,64,128]{2,1,0:T(8,128)(2,1)S(1)}, bf16[8,64,128]{2,1,0:T(8,128)(2,1)S(1)}, u32[]{:S(2)}, u32[]{:S(2)}) collective-permute-start(bf16[8,64,128]{2,1,0:T(8,128)(2,1)S(1)} %get-tuple-element.43), channel_id=1, source_target_pairs={{0,120},{8,0},{16,8},{24,16},{32,24},{40,32},{48,40},{56,48},{64,5... | collective-permute-start | bytes 393224 | tf_op jit(solution)/shard_map/ppermute | solution.py:183
  59.2 0.6 collective-permute-start.7
  59.8 1.3 %collective-permute-start.8 = (bf16[8,64,128]{2,1,0:T(8,128)(2,1)S(1)}, bf16[8,64,128]{2,1,0:T(8,128)(2,1)S(1)}, u32[]{:S(2)}, u32[]{:S(2)}) collective-permute-start(bf16[8,64,128]{2,1,0:T(8,128)(2,1)S(1)} %get-tuple-element.40), channel_id=1, source_target_pairs={{0,4},{1,5},{2,6},{3,7},{4,0},{5,1},{6,2},{7,3},{8,12},{9,13},{10,... | collective-permute-start | bytes 393224 | tf_op jit(solution)/shard_map/ppermute | solution.py:176
  61.1 2.8 %collective-permute-start.9 = (bf16[8,64,128]{2,1,0:T(8,128)(2,1)S(1)}, bf16[8,64,128]{2,1,0:T(8,128)(2,1)S(1)}, u32[]{:S(2)}, u32[]{:S(2)}) collective-permute-start(bf16[8,64,128]{2,1,0:T(8,128)(2,1)S(1)} %get-tuple-element.41), channel_id=1, source_target_pairs={{0,6},{1,7},{2,4},{3,5},{4,2},{5,3},{6,0},{7,1},{8,14},{9,15},{10,... | collective-permute-start | bytes 393224 | tf_op jit(solution)/shard_map/ppermute | solution.py:176
  63.9 1.7 %collective-permute-done.7.rest_0_ = bf16[8,64,128]{2,1,0:T(8,128)(2,1)S(1)} collective-permute-done((bf16[8,64,128]{2,1,0:T(8,128)(2,1)S(1)}, bf16[8,64,128]{2,1,0:T(8,128)(2,1)S(1)}, u32[]{:S(2)}, u32[]{:S(2)}) %collective-permute-start.7) | collective-permute-done | bytes 131104 | tf_op jit(solution)/shard_map/ppermute | solution.py:176
  65.6 1.4 %collective-permute-done.8.rest_1_ = bf16[8,64,128]{2,1,0:T(8,128)(2,1)S(1)} collective-permute-done((bf16[8,64,128]{2,1,0:T(8,128)(2,1)S(1)}, bf16[8,64,128]{2,1,0:T(8,128)(2,1)S(1)}, u32[]{:S(2)}, u32[]{:S(2)}) %collective-permute-start.8) | collective-permute-done | bytes 131104 | tf_op jit(solution)/shard_map/ppermute | solution.py:176
  67.0 2.2 %collective-permute-done.9.rest_2_ = bf16[8,64,128]{2,1,0:T(8,128)(2,1)S(1)} collective-permute-done((bf16[8,64,128]{2,1,0:T(8,128)(2,1)S(1)}, bf16[8,64,128]{2,1,0:T(8,128)(2,1)S(1)}, u32[]{:S(2)}, u32[]{:S(2)}) %collective-permute-start.9) | collective-permute-done | bytes 131104 | tf_op jit(solution)/shard_map/ppermute | solution.py:176
  69.1 3.9 %second_step.1 = (bf16[80,64,128]{2,1,0:T(8,128)(2,1)S(1)}, bf16[32,64,128]{2,1,0:T(8,128)(2,1)}) custom-call(s32[16,32]{1,0:T(8,128)S(1)} %bitcast.13, s32[1]{0:T(128)S(6)} %copy.19.count, bf16[32,64,1024]{2,1,0:T(8,128)(2,1)S(1)} %get-tuple-element.25.weights, bf16[2048,128]{1,0:T(8,128)(2,1)S(1)} %get-tuple-element.26.interp, ...), custom_call_target="tpu_custom_call", output_to_operand_aliasing={{0}: (8, {})} | custom-call | tf_op jit(solution)/shard_map/second_step/pallas_call | solution.py:385
  (17 shorter events, 0.2 us)
Async XLA Ops:
  2.3 42.0 %all-to-all-start = ((bf16[128,64,128]{2,1,0:T(8,128)(2,1)}), bf16[128,64,128]{2,1,0:T(8,128)(2,1)S(1)}, u32[]{:S(2)}, u32[]{:S(2)}) async-start(bf16[128,64,128]{2,1,0:T(8,128)(2,1)} %pick.1.after), calls=%async_computation | async-start | bytes 4194304 | tf_op jit(solution)/shard_map/all_to_all | solution.py:421
  13.5 3.5 %copy-start = (bf16[32,64,128]{2,1,0:T(8,128)(2,1)S(1)}, bf16[32,64,128]{2,1,0:T(8,128)(2,1)}, u32[]{:S(2)}) copy-start(bf16[32,64,128]{2,1,0:T(8,128)(2,1)} %latent.5) | copy-start | bytes 1572868
  13.5 3.5 %copy-start.1 = (s32[1,8,4]{1,2,0:T(4,128)S(1)}, s32[1,8,4]{1,2,0:T(4,128)}, u32[]{:S(2)}) copy-start(s32[1,8,4]{1,2,0:T(4,128)} %param.21) | copy-start | bytes 388
  13.5 3.5 %copy-start.3 = (s32[1,2,8]{2,1,0:T(2,128)S(1)}, s32[1,2,8]{2,1,0:T(2,128)}, u32[]{:S(2)}) copy-start(s32[1,2,8]{2,1,0:T(2,128)} %param.22) | copy-start | bytes 196
  15.4 1.6 %collective-permute-start = (bf16[16,64,128]{2,1,0:T(8,128)(2,1)S(1)}, bf16[16,64,128]{2,1,0:T(8,128)(2,1)S(1)}, u32[]{:S(2)}, u32[]{:S(2)}) collective-permute-start(bf16[16,64,128]{2,1,0:T(8,128)(2,1)S(1)} %first_hop.1), channel_id=1, source_target_pairs={{0,1},{1,0},{2,3},{3,2},{4,5},{5,4},{6,7},{7,6},{8,9},{9,8},{10,11... | collective-permute-start | bytes 786440 | tf_op jit(solution)/shard_map/ppermute | solution.py:170
  18.4 29.8 %collective-permute-start.1 = (bf16[8,64,128]{2,1,0:T(8,128)(2,1)}, bf16[8,64,128]{2,1,0:T(8,128)(2,1)S(1)}, u32[]{:S(2)}, u32[]{:S(2)}) collective-permute-start(bf16[8,64,128]{2,1,0:T(8,128)(2,1)} %get-tuple-element.32), channel_id=1, source_target_pairs={{0,2},{1,3},{2,0},{3,1},{4,6},{5,7},{6,4},{7,5},{8,10},{9,11},{10,... | collective-permute-start | bytes 393224 | tf_op jit(solution)/shard_map/ppermute | solution.py:176
  19.3 28.9 %collective-permute-start.2 = (bf16[8,64,128]{2,1,0:T(8,128)(2,1)S(1)}, bf16[8,64,128]{2,1,0:T(8,128)(2,1)S(1)}, u32[]{:S(2)}, u32[]{:S(2)}) collective-permute-start(bf16[8,64,128]{2,1,0:T(8,128)(2,1)S(1)} %get-tuple-element.33), channel_id=1, source_target_pairs={{0,4},{1,5},{2,6},{3,7},{4,0},{5,1},{6,2},{7,3},{8,12},{9,13},{10,... | collective-permute-start | bytes 393224 | tf_op jit(solution)/shard_map/ppermute | solution.py:176
  22.0 26.2 %collective-permute-start.3 = (bf16[8,64,128]{2,1,0:T(8,128)(2,1)S(1)}, bf16[8,64,128]{2,1,0:T(8,128)(2,1)S(1)}, u32[]{:S(2)}, u32[]{:S(2)}) collective-permute-start(bf16[8,64,128]{2,1,0:T(8,128)(2,1)S(1)} %get-tuple-element.34), channel_id=1, source_target_pairs={{0,6},{1,7},{2,4},{3,5},{4,2},{5,3},{6,0},{7,1},{8,14},{9,15},{10,... | collective-permute-start | bytes 393224 | tf_op jit(solution)/shard_map/ppermute | solution.py:176
  23.1 25.1 %collective-permute-start.4 = (bf16[8,64,128]{2,1,0:T(8,128)(2,1)S(1)}, bf16[8,64,128]{2,1,0:T(8,128)(2,1)S(1)}, u32[]{:S(2)}, u32[]{:S(2)}) collective-permute-start(bf16[8,64,128]{2,1,0:T(8,128)(2,1)S(1)} %get-tuple-element.35), channel_id=1, source_target_pairs={{0,8},{8,16},{16,24},{24,32},{32,40},{40,48},{48,56},{56,64},{64,7... | collective-permute-start | bytes 393224 | tf_op jit(solution)/shard_map/ppermute | solution.py:183
  24.1 24.1 %collective-permute-start.5 = (bf16[8,64,128]{2,1,0:T(8,128)(2,1)S(1)}, bf16[8,64,128]{2,1,0:T(8,128)(2,1)S(1)}, u32[]{:S(2)}, u32[]{:S(2)}) collective-permute-start(bf16[8,64,128]{2,1,0:T(8,128)(2,1)S(1)} %get-tuple-element.36), channel_id=1, source_target_pairs={{0,120},{8,0},{16,8},{24,16},{32,24},{40,32},{48,40},{56,48},{64,5... | collective-permute-start | bytes 393224 | tf_op jit(solution)/shard_map/ppermute | solution.py:183
  44.4 3.8 %copy-start.2 = (s32[32,16]{0,1:T(8,128)S(1)}, s32[32,16]{0,1:T(8,128)}, u32[]{:S(2)}) copy-start(s32[32,16]{0,1:T(8,128)} %param.16) | copy-start | bytes 6148
  51.5 1.6 %collective-permute-start.6 = (bf16[16,64,128]{2,1,0:T(8,128)(2,1)S(1)}, bf16[16,64,128]{2,1,0:T(8,128)(2,1)S(1)}, u32[]{:S(2)}, u32[]{:S(2)}) collective-permute-start(bf16[16,64,128]{2,1,0:T(8,128)(2,1)S(1)} %get-tuple-element.38), channel_id=1, source_target_pairs={{0,1},{1,0},{2,3},{3,2},{4,5},{5,4},{6,7},{7,6},{8,9},{9,8},{10,11... | collective-permute-start | bytes 786440 | tf_op jit(solution)/shard_map/ppermute | solution.py:170
  53.8 10.1 %collective-permute-start.10 = (bf16[8,64,128]{2,1,0:T(8,128)(2,1)S(1)}, bf16[8,64,128]{2,1,0:T(8,128)(2,1)S(1)}, u32[]{:S(2)}, u32[]{:S(2)}) collective-permute-start(bf16[8,64,128]{2,1,0:T(8,128)(2,1)S(1)} %get-tuple-element.42), channel_id=1, source_target_pairs={{0,8},{8,16},{16,24},{24,32},{32,40},{40,48},{48,56},{56,64},{64,7... | collective-permute-start | bytes 393224 | tf_op jit(solution)/shard_map/ppermute | solution.py:183
  54.4 9.4 %collective-permute-start.11 = (bf16[8,64,128]{2,1,0:T(8,128)(2,1)S(1)}, bf16[8,64,128]{2,1,0:T(8,128)(2,1)S(1)}, u32[]{:S(2)}, u32[]{:S(2)}) collective-permute-start(bf16[8,64,128]{2,1,0:T(8,128)(2,1)S(1)} %get-tuple-element.43), channel_id=1, source_target_pairs={{0,120},{8,0},{16,8},{24,16},{32,24},{40,32},{48,40},{56,48},{64,5... | collective-permute-start | bytes 393224 | tf_op jit(solution)/shard_map/ppermute | solution.py:183
  59.2 6.4 %collective-permute-start.7 = (bf16[8,64,128]{2,1,0:T(8,128)(2,1)S(1)}, bf16[8,64,128]{2,1,0:T(8,128)(2,1)S(1)}, u32[]{:S(2)}, u32[]{:S(2)}) collective-permute-start(bf16[8,64,128]{2,1,0:T(8,128)(2,1)S(1)} %get-tuple-element.39), channel_id=1, source_target_pairs={{0,2},{1,3},{2,0},{3,1},{4,6},{5,7},{6,4},{7,5},{8,10},{9,11},{10,... | collective-permute-start | bytes 393224 | tf_op jit(solution)/shard_map/ppermute | solution.py:176
  59.8 7.2 %collective-permute-start.8 = (bf16[8,64,128]{2,1,0:T(8,128)(2,1)S(1)}, bf16[8,64,128]{2,1,0:T(8,128)(2,1)S(1)}, u32[]{:S(2)}, u32[]{:S(2)}) collective-permute-start(bf16[8,64,128]{2,1,0:T(8,128)(2,1)S(1)} %get-tuple-element.40), channel_id=1, source_target_pairs={{0,4},{1,5},{2,6},{3,7},{4,0},{5,1},{6,2},{7,3},{8,12},{9,13},{10,... | collective-permute-start | bytes 393224 | tf_op jit(solution)/shard_map/ppermute | solution.py:176
  61.1 8.0 %collective-permute-start.9 = (bf16[8,64,128]{2,1,0:T(8,128)(2,1)S(1)}, bf16[8,64,128]{2,1,0:T(8,128)(2,1)S(1)}, u32[]{:S(2)}, u32[]{:S(2)}) collective-permute-start(bf16[8,64,128]{2,1,0:T(8,128)(2,1)S(1)} %get-tuple-element.41), channel_id=1, source_target_pairs={{0,6},{1,7},{2,4},{3,5},{4,2},{5,3},{6,0},{7,1},{8,14},{9,15},{10,... | collective-permute-start | bytes 393224 | tf_op jit(solution)/shard_map/ppermute | solution.py:176

commit v3 on v2

--- a/solution.py
+++ b/solution.py
@@ -358,7 +358,8 @@
 ):
     del pool_in
     ways = sub_shape.shape[1] // CORES - 1
-    pieces, (below, above, *rest) = rest[:ways], rest[ways:]
+    last, below, above, *rest = rest
+    pieces, rest = [*rest[: ways - 1], last], rest[ways - 1 :]
     pool, out, summed, staged, out_sems = rest
     blocks, rows, lat = staged.shape
     fill_pool(pool, blocks, sub_shape, passed, pieces, below, above)
@@ -381,6 +382,7 @@
 def second_step(pool, halo, weights, interp, ids, network, count, sub_ids):
     rows, lat = pool.shape[1:]
     blocks = weights.shape[0]
+    passed, *pieces, below, above = halo
     operands = [ids, count, *map(in_vmem, (weights, interp, *network, pool))]
     return pl.pallas_call(
         second_kernel,
@@ -395,7 +397,7 @@
         ],
         compiler_params=params(16),
         name="second_step",
-    )(*operands, sub_ids, *halo)[1]
+    )(*operands, sub_ids, passed, *pieces[-1:], below, above, *pieces[:-1])[1]
 
 
 def per_device(

time: 73.8 us -> 71.2 us (0.965)
  waiting for transfers between devices: 23.6 us -> 21.3 us
    ppermute x6, waiting for transfers between devices: 5.24 us -> 0.54 us  [along_x(): lax.ppermute(piece, 'sub', [(i, i ^ way * CORES) for i in range(size)])]
    ppermute x4, waiting for transfers between devices: 0.01 us -> 2.42 us  [along_dom(): lax.ppermute(blocks, 'dom', [(i, (i + distance) % size) for i in range(si...]
  transfers between devices with their start and end apart: 13 -> 13, of which waited for: 6 -> 5; matrix products, arithmetic and copies ran while one was open for 0% -> 0% of each run, Pallas kernels for 10% -> 10%
where the time goes in v3:
time: 71.2 us; the launch traced here: 70.7 us
  starting transfers between devices  31.5 us (44%)
  waiting for transfers between devices  21.3 us (30%)
  Pallas kernels  17.1 us (24%)
  between operations  0.8 us (1%)
    all_to_all x1, waiting for transfers between devices, per_device(): lax.all_to_all(payload, ('dom', 'sub'), split_axis=0, concat_axis=0, tile...  15.3 us
    all_to_all x1, starting transfers between devices, per_device(): lax.all_to_all(payload, ('dom', 'sub'), split_axis=0, concat_axis=0, tile...  11.1 us
    ppermute x4, starting transfers between devices, along_dom(): lax.ppermute(blocks, 'dom', [(i, (i + distance) % size) for i in range(si...  10.7 us
    ppermute x6, starting transfers between devices, along_x(): lax.ppermute(piece, 'sub', [(i, i ^ way * CORES) for i in range(size)])  9.48 us
    pallas_call x1, Pallas kernels, second_step(): pl.pallas_call(second_kernel, in_specs=[SMEM] * 2 + [VMEM] * 7 + [ANY] +...  3.91 us
    pallas_call x1, Pallas kernels, prepare(): pl.pallas_call(prepare_kernel, in_specs=[ANY, VMEM] + [ANY] * 7, out_spec...  3.76 us
    pallas_call x1, Pallas kernels, first_step(): pl.pallas_call(first_kernel, in_specs=[SMEM] * 3 + [VMEM] * (7 + len(halo...  3.3 us
    ppermute x2, waiting for transfers between devices, to_other_core(): lax.ppermute(blocks, 'sub', [(i, i ^ 1) for i in range(lax.axis_size('sub...  3.04 us
  transfers between devices with their start and end apart: 13, of which 5 were waited for; matrix products, arithmetic and copies ran while one was open for 0% of the time, Pallas kernels for 10%

profile of v3, /device:TPU:0, one launch (start us, length us, event | category | flops | bytes accessed | tf_op | source)
XLA Modules:
  0.0 70.7 jit_solution(2610906382435453608)
XLA Ops:
  0.0 2.3 %pick.1.after = bf16[128,64,128]{2,1,0:T(8,128)(2,1)} custom-call(s32[1,128]{1,0:T(1,128)} %bitcast.17, bf16[8,64,128]{2,1,0:T(8,128)(2,1)} %table.1), custom_call_target="tpu_custom_call" | custom-call | tf_op jit(solution)/shard_map/pick/pallas_call | solution.py:133
  2.3 11.1 %all-to-all-start = ((bf16[128,64,128]{2,1,0:T(8,128)(2,1)}), bf16[128,64,128]{2,1,0:T(8,128)(2,1)S(1)}, u32[]{:S(2)}, u32[]{:S(2)}) async-start(bf16[128,64,128]{2,1,0:T(8,128)(2,1)} %pick.1.after), calls=%async_computation | async-start | bytes 4194304 | tf_op jit(solution)/shard_map/all_to_all | solution.py:423
  13.5 1.9 %first_hop.1 = bf16[16,64,128]{2,1,0:T(8,128)(2,1)S(1)} custom-call(s32[4,8]{1,0:T(4,128)} %bitcast.7, bf16[32,64,128]{2,1,0:T(8,128)(2,1)} %latent.5, bf16[128,64,128]{2,1,0:T(8,128)(2,1)} %pick.1.after), custom_call_target="tpu_custom_call" | custom-call | tf_op jit(solution)/shard_map/first_hop/pallas_call | solution.py:99
  15.5 1.5 %collective-permute-done.passed = bf16[16,64,128]{2,1,0:T(8,128)(2,1)S(1)} collective-permute-done((bf16[16,64,128]{2,1,0:T(8,128)(2,1)S(1)}, bf16[16,64,128]{2,1,0:T(8,128)(2,1)S(1)}, u32[]{:S(2)}, u32[]{:S(2)}) %collective-permute-start) | collective-permute-done | bytes 262176 | tf_op jit(solution)/shard_map/ppermute | solution.py:170
  17.0 1.3 %repack.2 = (bf16[8,64,128]{2,1,0:T(8,128)(2,1)}, bf16[8,64,128]{2,1,0:T(8,128)(2,1)S(1)}, bf16[8,64,128]{2,1,0:T(8,128)(2,1)S(1)}, bf16[8,64,128]{2,1,0:T(8,128)(2,1)S(1)}, bf16[8,64,128]{2,1,0:T(8,128)(2,1)S(1)}) custom-call(s32[4,8]{1,0:T(4,128)S(1)} %bitcast.8, s32[2,8]{1,0:T(2,128)S(1)} %bitcast.14, bf16[32,64,128]{2,1,0:T(8,128)(2,1)S(1)} %copy-done, ...), custom_call_target="tpu_custom_call" | custom-call | tf_op jit(solution)/shard_map/repack/pallas_call | solution.py:159
  18.3 1.0 %collective-permute-start.1 = (bf16[8,64,128]{2,1,0:T(8,128)(2,1)}, bf16[8,64,128]{2,1,0:T(8,128)(2,1)S(1)}, u32[]{:S(2)}, u32[]{:S(2)}) collective-permute-start(bf16[8,64,128]{2,1,0:T(8,128)(2,1)} %get-tuple-element.32), channel_id=1, source_target_pairs={{0,2},{1,3},{2,0},{3,1},{4,6},{5,7},{6,4},{7,5},{8,10},{9,11},{10,... | collective-permute-start | bytes 393224 | tf_op jit(solution)/shard_map/ppermute | solution.py:176
  19.3 2.7 %collective-permute-start.2 = (bf16[8,64,128]{2,1,0:T(8,128)(2,1)S(1)}, bf16[8,64,128]{2,1,0:T(8,128)(2,1)S(1)}, u32[]{:S(2)}, u32[]{:S(2)}) collective-permute-start(bf16[8,64,128]{2,1,0:T(8,128)(2,1)S(1)} %get-tuple-element.33), channel_id=1, source_target_pairs={{0,4},{1,5},{2,6},{3,7},{4,0},{5,1},{6,2},{7,3},{8,12},{9,13},{10,... | collective-permute-start | bytes 393224 | tf_op jit(solution)/shard_map/ppermute | solution.py:176
  22.0 1.1 %collective-permute-start.3 = (bf16[8,64,128]{2,1,0:T(8,128)(2,1)S(1)}, bf16[8,64,128]{2,1,0:T(8,128)(2,1)S(1)}, u32[]{:S(2)}, u32[]{:S(2)}) collective-permute-start(bf16[8,64,128]{2,1,0:T(8,128)(2,1)S(1)} %get-tuple-element.34), channel_id=1, source_target_pairs={{0,6},{1,7},{2,4},{3,5},{4,2},{5,3},{6,0},{7,1},{8,14},{9,15},{10,... | collective-permute-start | bytes 393224 | tf_op jit(solution)/shard_map/ppermute | solution.py:176
  23.0 1.1 %collective-permute-start.4 = (bf16[8,64,128]{2,1,0:T(8,128)(2,1)S(1)}, bf16[8,64,128]{2,1,0:T(8,128)(2,1)S(1)}, u32[]{:S(2)}, u32[]{:S(2)}) collective-permute-start(bf16[8,64,128]{2,1,0:T(8,128)(2,1)S(1)} %get-tuple-element.35), channel_id=1, source_target_pairs={{0,8},{8,16},{16,24},{24,32},{32,40},{40,48},{48,56},{56,64},{64,7... | collective-permute-start | bytes 393224 | tf_op jit(solution)/shard_map/ppermute | solution.py:183
  24.1 4.3 %collective-permute-start.5 = (bf16[8,64,128]{2,1,0:T(8,128)(2,1)S(1)}, bf16[8,64,128]{2,1,0:T(8,128)(2,1)S(1)}, u32[]{:S(2)}, u32[]{:S(2)}) collective-permute-start(bf16[8,64,128]{2,1,0:T(8,128)(2,1)S(1)} %get-tuple-element.36), channel_id=1, source_target_pairs={{0,120},{8,0},{16,8},{24,16},{32,24},{40,32},{48,40},{56,48},{64,5... | collective-permute-start | bytes 393224 | tf_op jit(solution)/shard_map/ppermute | solution.py:183
  29.0 15.3 %all-to-all-done.received = bf16[128,64,128]{2,1,0:T(8,128)(2,1)S(1)} async-done(((bf16[128,64,128]{2,1,0:T(8,128)(2,1)}), bf16[128,64,128]{2,1,0:T(8,128)(2,1)S(1)}, u32[]{:S(2)}, u32[]{:S(2)}) %all-to-all-start) | async-done | bytes 2097184 | tf_op jit(solution)/shard_map/all_to_all | solution.py:423
  44.4 3.8 %prepare.1 = (bf16[2048,128]{1,0:T(8,128)(2,1)S(1)}, bf16[32,64,1024]{2,1,0:T(8,128)(2,1)S(1)}, bf16[80,64,128]{2,1,0:T(8,128)(2,1)S(1)}, bf16[2,384,128]{2,1,0:...) custom-call(s32[4,32]{1,0:T(4,128)} %bitcast.16, ...), custom_call_target="tpu_custom_call" | custom-call | tf_op jit(solution)/shard_map/prepare/pallas_call | solution.py:292
  48.2 3.3 %first_step.1 = (bf16[80,64,128]{2,1,0:T(8,128)(2,1)S(1)}, bf16[16,64,128]{2,1,0:T(8,128)(2,1)S(1)}) custom-call(s32[1]{0:T(128)S(6)} %copy.19.count, s32[16,32]{1,0:T(8,128)S(1)} %bitcast.12, s32[4,8]{1,0:T(4,128)S(1)} %bitcast.9, bf16[32,64,1024]{2,1,0:T(8,128)(2,1)S(1)} %get-tuple-element.25.weights, ...), custom_call_target="tpu_custom_call", output_to_operand_aliasing={{0}: (9, {})} | custom-call | tf_op jit(solution)/shard_map/first_step/pallas_call | solution.py:341
  51.5 0.1 collective-permute-start.6
  51.6 1.5 %collective-permute-done.6.passed = bf16[16,64,128]{2,1,0:T(8,128)(2,1)S(1)} collective-permute-done((bf16[16,64,128]{2,1,0:T(8,128)(2,1)S(1)}, bf16[16,64,128]{2,1,0:T(8,128)(2,1)S(1)}, u32[]{:S(2)}, u32[]{:S(2)}) %collective-permute-start.6) | collective-permute-done | bytes 262176 | tf_op jit(solution)/shard_map/ppermute | solution.py:170
  53.1 0.6 repack.3
  53.8 0.7 collective-permute-start.10
  54.4 1.3 %collective-permute-start.11 = (bf16[8,64,128]{2,1,0:T(8,128)(2,1)S(1)}, bf16[8,64,128]{2,1,0:T(8,128)(2,1)S(1)}, u32[]{:S(2)}, u32[]{:S(2)}) collective-permute-start(bf16[8,64,128]{2,1,0:T(8,128)(2,1)S(1)} %get-tuple-element.43), channel_id=1, source_target_pairs={{0,4},{1,5},{2,6},{3,7},{4,0},{5,1},{6,2},{7,3},{8,12},{9,13},{10,... | collective-permute-start | bytes 393224 | tf_op jit(solution)/shard_map/ppermute | solution.py:176
  55.7 2.8 %collective-permute-start.7 = (bf16[8,64,128]{2,1,0:T(8,128)(2,1)S(1)}, bf16[8,64,128]{2,1,0:T(8,128)(2,1)S(1)}, u32[]{:S(2)}, u32[]{:S(2)}) collective-permute-start(bf16[8,64,128]{2,1,0:T(8,128)(2,1)S(1)} %get-tuple-element.39), channel_id=1, source_target_pairs={{0,6},{1,7},{2,4},{3,5},{4,2},{5,3},{6,0},{7,1},{8,14},{9,15},{10,... | collective-permute-start | bytes 393224 | tf_op jit(solution)/shard_map/ppermute | solution.py:176
  58.5 0.6 collective-permute-start.8
  59.2 4.7 %collective-permute-start.9 = (bf16[8,64,128]{2,1,0:T(8,128)(2,1)S(1)}, bf16[8,64,128]{2,1,0:T(8,128)(2,1)S(1)}, u32[]{:S(2)}, u32[]{:S(2)}) collective-permute-start(bf16[8,64,128]{2,1,0:T(8,128)(2,1)S(1)} %get-tuple-element.41), channel_id=1, source_target_pairs={{0,120},{8,0},{16,8},{24,16},{32,24},{40,32},{48,40},{56,48},{64,5... | collective-permute-start | bytes 393224 | tf_op jit(solution)/shard_map/ppermute | solution.py:183
  63.9 0.5 collective-permute-done.7.rest_0_
  64.4 2.4 %collective-permute-done.8.rest_1_ = bf16[8,64,128]{2,1,0:T(8,128)(2,1)S(1)} collective-permute-done((bf16[8,64,128]{2,1,0:T(8,128)(2,1)S(1)}, bf16[8,64,128]{2,1,0:T(8,128)(2,1)S(1)}, u32[]{:S(2)}, u32[]{:S(2)}) %collective-permute-start.8) | collective-permute-done | bytes 131104 | tf_op jit(solution)/shard_map/ppermute | solution.py:183
  66.8 3.9 %second_step.1 = (bf16[80,64,128]{2,1,0:T(8,128)(2,1)S(1)}, bf16[32,64,128]{2,1,0:T(8,128)(2,1)}) custom-call(s32[16,32]{1,0:T(8,128)S(1)} %bitcast.13, s32[1]{0:T(128)S(6)} %copy.19.count, bf16[32,64,1024]{2,1,0:T(8,128)(2,1)S(1)} %get-tuple-element.25.weights, bf16[2048,128]{1,0:T(8,128)(2,1)S(1)} %get-tuple-element.26.interp, ...), custom_call_target="tpu_custom_call", output_to_operand_aliasing={{0}: (8, {})} | custom-call | tf_op jit(solution)/shard_map/second_step/pallas_call | solution.py:387
  (17 shorter events, 0.1 us)
Async XLA Ops:
  2.3 42.0 %all-to-all-start = ((bf16[128,64,128]{2,1,0:T(8,128)(2,1)}), bf16[128,64,128]{2,1,0:T(8,128)(2,1)S(1)}, u32[]{:S(2)}, u32[]{:S(2)}) async-start(bf16[128,64,128]{2,1,0:T(8,128)(2,1)} %pick.1.after), calls=%async_computation | async-start | bytes 4194304 | tf_op jit(solution)/shard_map/all_to_all | solution.py:423
  13.5 3.5 %copy-start = (bf16[32,64,128]{2,1,0:T(8,128)(2,1)S(1)}, bf16[32,64,128]{2,1,0:T(8,128)(2,1)}, u32[]{:S(2)}) copy-start(bf16[32,64,128]{2,1,0:T(8,128)(2,1)} %latent.5) | copy-start | bytes 1572868
  13.5 3.5 %copy-start.1 = (s32[1,8,4]{1,2,0:T(4,128)S(1)}, s32[1,8,4]{1,2,0:T(4,128)}, u32[]{:S(2)}) copy-start(s32[1,8,4]{1,2,0:T(4,128)} %param.21) | copy-start | bytes 388
  13.5 3.5 %copy-start.3 = (s32[1,2,8]{2,1,0:T(2,128)S(1)}, s32[1,2,8]{2,1,0:T(2,128)}, u32[]{:S(2)}) copy-start(s32[1,2,8]{2,1,0:T(2,128)} %param.22) | copy-start | bytes 196
  15.4 1.6 %collective-permute-start = (bf16[16,64,128]{2,1,0:T(8,128)(2,1)S(1)}, bf16[16,64,128]{2,1,0:T(8,128)(2,1)S(1)}, u32[]{:S(2)}, u32[]{:S(2)}) collective-permute-start(bf16[16,64,128]{2,1,0:T(8,128)(2,1)S(1)} %first_hop.1), channel_id=1, source_target_pairs={{0,1},{1,0},{2,3},{3,2},{4,5},{5,4},{6,7},{7,6},{8,9},{9,8},{10,11... | collective-permute-start | bytes 786440 | tf_op jit(solution)/shard_map/ppermute | solution.py:170
  18.3 29.8 %collective-permute-start.1 = (bf16[8,64,128]{2,1,0:T(8,128)(2,1)}, bf16[8,64,128]{2,1,0:T(8,128)(2,1)S(1)}, u32[]{:S(2)}, u32[]{:S(2)}) collective-permute-start(bf16[8,64,128]{2,1,0:T(8,128)(2,1)} %get-tuple-element.32), channel_id=1, source_target_pairs={{0,2},{1,3},{2,0},{3,1},{4,6},{5,7},{6,4},{7,5},{8,10},{9,11},{10,... | collective-permute-start | bytes 393224 | tf_op jit(solution)/shard_map/ppermute | solution.py:176
  19.3 28.8 %collective-permute-start.2 = (bf16[8,64,128]{2,1,0:T(8,128)(2,1)S(1)}, bf16[8,64,128]{2,1,0:T(8,128)(2,1)S(1)}, u32[]{:S(2)}, u32[]{:S(2)}) collective-permute-start(bf16[8,64,128]{2,1,0:T(8,128)(2,1)S(1)} %get-tuple-element.33), channel_id=1, source_target_pairs={{0,4},{1,5},{2,6},{3,7},{4,0},{5,1},{6,2},{7,3},{8,12},{9,13},{10,... | collective-permute-start | bytes 393224 | tf_op jit(solution)/shard_map/ppermute | solution.py:176
  22.0 26.2 %collective-permute-start.3 = (bf16[8,64,128]{2,1,0:T(8,128)(2,1)S(1)}, bf16[8,64,128]{2,1,0:T(8,128)(2,1)S(1)}, u32[]{:S(2)}, u32[]{:S(2)}) collective-permute-start(bf16[8,64,128]{2,1,0:T(8,128)(2,1)S(1)} %get-tuple-element.34), channel_id=1, source_target_pairs={{0,6},{1,7},{2,4},{3,5},{4,2},{5,3},{6,0},{7,1},{8,14},{9,15},{10,... | collective-permute-start | bytes 393224 | tf_op jit(solution)/shard_map/ppermute | solution.py:176
  23.0 25.1 %collective-permute-start.4 = (bf16[8,64,128]{2,1,0:T(8,128)(2,1)S(1)}, bf16[8,64,128]{2,1,0:T(8,128)(2,1)S(1)}, u32[]{:S(2)}, u32[]{:S(2)}) collective-permute-start(bf16[8,64,128]{2,1,0:T(8,128)(2,1)S(1)} %get-tuple-element.35), channel_id=1, source_target_pairs={{0,8},{8,16},{16,24},{24,32},{32,40},{40,48},{48,56},{56,64},{64,7... | collective-permute-start | bytes 393224 | tf_op jit(solution)/shard_map/ppermute | solution.py:183
  24.1 24.1 %collective-permute-start.5 = (bf16[8,64,128]{2,1,0:T(8,128)(2,1)S(1)}, bf16[8,64,128]{2,1,0:T(8,128)(2,1)S(1)}, u32[]{:S(2)}, u32[]{:S(2)}) collective-permute-start(bf16[8,64,128]{2,1,0:T(8,128)(2,1)S(1)} %get-tuple-element.36), channel_id=1, source_target_pairs={{0,120},{8,0},{16,8},{24,16},{32,24},{40,32},{48,40},{56,48},{64,5... | collective-permute-start | bytes 393224 | tf_op jit(solution)/shard_map/ppermute | solution.py:183
  44.4 3.8 %copy-start.2 = (s32[32,16]{0,1:T(8,128)S(1)}, s32[32,16]{0,1:T(8,128)}, u32[]{:S(2)}) copy-start(s32[32,16]{0,1:T(8,128)} %param.16) | copy-start | bytes 6148
  51.5 1.6 %collective-permute-start.6 = (bf16[16,64,128]{2,1,0:T(8,128)(2,1)S(1)}, bf16[16,64,128]{2,1,0:T(8,128)(2,1)S(1)}, u32[]{:S(2)}, u32[]{:S(2)}) collective-permute-start(bf16[16,64,128]{2,1,0:T(8,128)(2,1)S(1)} %get-tuple-element.38), channel_id=1, source_target_pairs={{0,1},{1,0},{2,3},{3,2},{4,5},{5,4},{6,7},{7,6},{8,9},{9,8},{10,11... | collective-permute-start | bytes 786440 | tf_op jit(solution)/shard_map/ppermute | solution.py:170
  53.8 10.1 %collective-permute-start.10 = (bf16[8,64,128]{2,1,0:T(8,128)(2,1)S(1)}, bf16[8,64,128]{2,1,0:T(8,128)(2,1)S(1)}, u32[]{:S(2)}, u32[]{:S(2)}) collective-permute-start(bf16[8,64,128]{2,1,0:T(8,128)(2,1)S(1)} %get-tuple-element.42), channel_id=1, source_target_pairs={{0,2},{1,3},{2,0},{3,1},{4,6},{5,7},{6,4},{7,5},{8,10},{9,11},{10,... | collective-permute-start | bytes 393224 | tf_op jit(solution)/shard_map/ppermute | solution.py:176
  54.4 9.5 %collective-permute-start.11 = (bf16[8,64,128]{2,1,0:T(8,128)(2,1)S(1)}, bf16[8,64,128]{2,1,0:T(8,128)(2,1)S(1)}, u32[]{:S(2)}, u32[]{:S(2)}) collective-permute-start(bf16[8,64,128]{2,1,0:T(8,128)(2,1)S(1)} %get-tuple-element.43), channel_id=1, source_target_pairs={{0,4},{1,5},{2,6},{3,7},{4,0},{5,1},{6,2},{7,3},{8,12},{9,13},{10,... | collective-permute-start | bytes 393224 | tf_op jit(solution)/shard_map/ppermute | solution.py:176
  55.7 8.7 %collective-permute-start.7 = (bf16[8,64,128]{2,1,0:T(8,128)(2,1)S(1)}, bf16[8,64,128]{2,1,0:T(8,128)(2,1)S(1)}, u32[]{:S(2)}, u32[]{:S(2)}) collective-permute-start(bf16[8,64,128]{2,1,0:T(8,128)(2,1)S(1)} %get-tuple-element.39), channel_id=1, source_target_pairs={{0,6},{1,7},{2,4},{3,5},{4,2},{5,3},{6,0},{7,1},{8,14},{9,15},{10,... | collective-permute-start | bytes 393224 | tf_op jit(solution)/shard_map/ppermute | solution.py:176
  58.5 8.3 %collective-permute-start.8 = (bf16[8,64,128]{2,1,0:T(8,128)(2,1)S(1)}, bf16[8,64,128]{2,1,0:T(8,128)(2,1)S(1)}, u32[]{:S(2)}, u32[]{:S(2)}) collective-permute-start(bf16[8,64,128]{2,1,0:T(8,128)(2,1)S(1)} %get-tuple-element.40), channel_id=1, source_target_pairs={{0,8},{8,16},{16,24},{24,32},{32,40},{40,48},{48,56},{56,64},{64,7... | collective-permute-start | bytes 393224 | tf_op jit(solution)/shard_map/ppermute | solution.py:183
  59.2 7.7 %collective-permute-start.9 = (bf16[8,64,128]{2,1,0:T(8,128)(2,1)S(1)}, bf16[8,64,128]{2,1,0:T(8,128)(2,1)S(1)}, u32[]{:S(2)}, u32[]{:S(2)}) collective-permute-start(bf16[8,64,128]{2,1,0:T(8,128)(2,1)S(1)} %get-tuple-element.41), channel_id=1, source_target_pairs={{0,120},{8,0},{16,8},{24,16},{32,24},{40,32},{48,40},{56,48},{64,5... | collective-permute-start | bytes 393224 | tf_op jit(solution)/shard_map/ppermute | solution.py:183

commit v4 on v1

--- a/solution.py
+++ b/solution.py
@@ -13,6 +13,7 @@
 VMEM = pl.BlockSpec(memory_space=pltpu.VMEM)
 ANY = pl.BlockSpec(memory_space=pl.ANY)
 CORES = 2
+WAYS = (1, 3, 2)
 AHEAD = 2
 
 
@@ -71,7 +72,7 @@
     slots = sub_ids.shape[0]
     me = lax.axis_index("sub")
     mine = (me % CORES) * slots
-    for way, out in enumerate(outs, 1):
+    for way, out in zip(WAYS, outs):
         for slot in range(slots):
             out[mine + slot] = latent[sub_ids[slot, me ^ (way * CORES)]]
             out[slots - mine + slot] = passed[way * slots + slot]
@@ -175,7 +176,7 @@
     size = lax.axis_size("sub")
     return [
         lax.ppermute(piece, "sub", [(i, i ^ (way * CORES)) for i in range(size)])
-        for way, piece in enumerate(pieces, 1)
+        for way, piece in zip(WAYS, pieces)
     ]
 
 
@@ -194,7 +195,7 @@
     slots, peers = sub_ids.shape
     me = lax.axis_index("sub")
     pool[pl.ds(own + (me ^ 1) * slots, slots)] = passed[:slots]
-    for way, piece in enumerate(pieces, 1):
+    for way, piece in zip(WAYS, pieces):
         first = own + (me // CORES ^ way) * CORES * slots
         pool[pl.ds(first, piece.shape[0])] = piece[...]
     end = own + peers * slots

time: 69.7 us -> 69.1 us (level)
  starting transfers between devices: 31.9 us -> 30.7 us
    ppermute x4, waiting for transfers between devices: 0.63 us -> 2.13 us  [along_dom(): lax.ppermute(blocks, 'dom', [(i, (i + distance) % size) for i in range(si...]
    ppermute x6, starting transfers between devices: 9.56 us -> 8.35 us  [along_x(): lax.ppermute(piece, 'sub', [(i, i ^ way * CORES) for i in range(size)])]
    ppermute x6, waiting for transfers between devices: 18.3 us -> 17.4 us  [along_x(): lax.ppermute(piece, 'sub', [(i, i ^ way * CORES) for i in range(size)])]
where the time goes in v4:
time: 69.1 us; the launch traced here: 68.7 us
  starting transfers between devices  30.7 us (44%)
  waiting for transfers between devices  22.5 us (33%)
  Pallas kernels  14.5 us (21%)
  between operations  0.83 us (1%)
    ppermute x6, waiting for transfers between devices, along_x(): lax.ppermute(piece, 'sub', [(i, i ^ way * CORES) for i in range(size)])  17.4 us
    all_to_all x1, starting transfers between devices, per_device(): lax.all_to_all(payload, ('dom', 'sub'), split_axis=0, concat_axis=0, tile...  11.1 us
    ppermute x4, starting transfers between devices, along_dom(): lax.ppermute(blocks, 'dom', [(i, (i + distance) % size) for i in range(si...  11 us
    ppermute x6, starting transfers between devices, along_x(): lax.ppermute(piece, 'sub', [(i, i ^ way * CORES) for i in range(size)])  8.35 us
    pallas_call x1, Pallas kernels, first_step(): pl.pallas_call(first_kernel, in_specs=[SMEM, ANY, ANY, ANY, VMEM] + [ANY]...  5.15 us
    pallas_call x1, Pallas kernels, second_step(): pl.pallas_call(second_kernel, in_specs=[SMEM] * 2 + [VMEM] * 7 + [ANY] +...  3.92 us
    ppermute x2, waiting for transfers between devices, to_other_core(): lax.ppermute(blocks, 'sub', [(i, i ^ 1) for i in range(lax.axis_size('sub...  3.04 us
    pallas_call x1, Pallas kernels, pick(): pl.pallas_call(pick_kernel, in_specs=[ANY, ANY], out_specs=ANY, out_shape...  2.34 us
  transfers between devices with their start and end apart: 13, of which 7 were waited for; matrix products, arithmetic and copies ran while one was open for 0% of the time, Pallas kernels for 4%

profile of v4, /device:TPU:0, one launch (start us, length us, event | category | flops | bytes accessed | tf_op | source)
XLA Modules:
  0.0 68.7 jit_solution(9921927061553823288)
XLA Ops:
  0.0 2.3 %pick.1.after = bf16[128,64,128]{2,1,0:T(8,128)(2,1)} custom-call(s32[1,128]{1,0:T(1,128)} %bitcast.17, bf16[8,64,128]{2,1,0:T(8,128)(2,1)} %table.1), custom_call_target="tpu_custom_call" | custom-call | tf_op jit(solution)/shard_map/pick/pallas_call | solution.py:135
  2.3 11.1 %all-to-all-start = ((bf16[128,64,128]{2,1,0:T(8,128)(2,1)}), bf16[128,64,128]{2,1,0:T(8,128)(2,1)S(1)}, u32[]{:S(2)}, u32[]{:S(2)}) async-start(bf16[128,64,128]{2,1,0:T(8,128)(2,1)} %pick.1.after), calls=%async_computation | async-start | bytes 4194304 | tf_op jit(solution)/shard_map/all_to_all | solution.py:422
  13.5 1.9 %first_hop.1 = bf16[16,64,128]{2,1,0:T(8,128)(2,1)S(1)} custom-call(s32[4,8]{1,0:T(4,128)} %bitcast.7, bf16[32,64,128]{2,1,0:T(8,128)(2,1)} %latent.5, bf16[128,64,128]{2,1,0:T(8,128)(2,1)} %pick.1.after), custom_call_target="tpu_custom_call" | custom-call | tf_op jit(solution)/shard_map/first_hop/pallas_call | solution.py:101
  15.5 1.5 %collective-permute-done.passed = bf16[16,64,128]{2,1,0:T(8,128)(2,1)S(1)} collective-permute-done((bf16[16,64,128]{2,1,0:T(8,128)(2,1)S(1)}, bf16[16,64,128]{2,1,0:T(8,128)(2,1)S(1)}, u32[]{:S(2)}, u32[]{:S(2)}) %collective-permute-start) | collective-permute-done | bytes 262176 | tf_op jit(solution)/shard_map/ppermute | solution.py:172
  17.0 0.6 repack.2
  17.7 1.1 %collective-permute-start.1 = (bf16[8,64,128]{2,1,0:T(8,128)(2,1)S(1)}, bf16[8,64,128]{2,1,0:T(8,128)(2,1)S(1)}, u32[]{:S(2)}, u32[]{:S(2)}) collective-permute-start(bf16[8,64,128]{2,1,0:T(8,128)(2,1)S(1)} %get-tuple-element.20), channel_id=1, source_target_pairs={{0,2},{1,3},{2,0},{3,1},{4,6},{5,7},{6,4},{7,5},{8,10},{9,11},{10,... | collective-permute-start | bytes 393224 | tf_op jit(solution)/shard_map/ppermute | solution.py:178
  18.7 2.1 %collective-permute-start.2 = (bf16[8,64,128]{2,1,0:T(8,128)(2,1)S(1)}, bf16[8,64,128]{2,1,0:T(8,128)(2,1)S(1)}, u32[]{:S(2)}, u32[]{:S(2)}) collective-permute-start(bf16[8,64,128]{2,1,0:T(8,128)(2,1)S(1)} %get-tuple-element.21), channel_id=1, source_target_pairs={{0,6},{1,7},{2,4},{3,5},{4,2},{5,3},{6,0},{7,1},{8,14},{9,15},{10,... | collective-permute-start | bytes 393224 | tf_op jit(solution)/shard_map/ppermute | solution.py:178
  20.8 1.0 %collective-permute-start.3 = (bf16[8,64,128]{2,1,0:T(8,128)(2,1)S(1)}, bf16[8,64,128]{2,1,0:T(8,128)(2,1)S(1)}, u32[]{:S(2)}, u32[]{:S(2)}) collective-permute-start(bf16[8,64,128]{2,1,0:T(8,128)(2,1)S(1)} %get-tuple-element.22), channel_id=1, source_target_pairs={{0,4},{1,5},{2,6},{3,7},{4,0},{5,1},{6,2},{7,3},{8,12},{9,13},{10,... | collective-permute-start | bytes 393224 | tf_op jit(solution)/shard_map/ppermute | solution.py:178
  21.9 1.2 %collective-permute-start.4 = (bf16[8,64,128]{2,1,0:T(8,128)(2,1)S(1)}, bf16[8,64,128]{2,1,0:T(8,128)(2,1)S(1)}, u32[]{:S(2)}, u32[]{:S(2)}) collective-permute-start(bf16[8,64,128]{2,1,0:T(8,128)(2,1)S(1)} %get-tuple-element.23), channel_id=1, source_target_pairs={{0,8},{8,16},{16,24},{24,32},{32,40},{40,48},{48,56},{56,64},{64,7... | collective-permute-start | bytes 393224 | tf_op jit(solution)/shard_map/ppermute | solution.py:185
  23.0 4.2 %collective-permute-start.5 = (bf16[8,64,128]{2,1,0:T(8,128)(2,1)S(1)}, bf16[8,64,128]{2,1,0:T(8,128)(2,1)S(1)}, u32[]{:S(2)}, u32[]{:S(2)}) collective-permute-start(bf16[8,64,128]{2,1,0:T(8,128)(2,1)S(1)} %get-tuple-element.24), channel_id=1, source_target_pairs={{0,120},{8,0},{16,8},{24,16},{32,24},{40,32},{48,40},{56,48},{64,5... | collective-permute-start | bytes 393224 | tf_op jit(solution)/shard_map/ppermute | solution.py:185
  27.9 12.7 %collective-permute-done.1.rest_0_ = bf16[8,64,128]{2,1,0:T(8,128)(2,1)S(1)} collective-permute-done((bf16[8,64,128]{2,1,0:T(8,128)(2,1)S(1)}, bf16[8,64,128]{2,1,0:T(8,128)(2,1)S(1)}, u32[]{:S(2)}, u32[]{:S(2)}) %collective-permute-start.1) | collective-permute-done | bytes 131104 | tf_op jit(solution)/shard_map/ppermute | solution.py:178
  40.5 0.9 %collective-permute-done.2.rest_1_ = bf16[8,64,128]{2,1,0:T(8,128)(2,1)S(1)} collective-permute-done((bf16[8,64,128]{2,1,0:T(8,128)(2,1)S(1)}, bf16[8,64,128]{2,1,0:T(8,128)(2,1)S(1)}, u32[]{:S(2)}, u32[]{:S(2)}) %collective-permute-start.2) | collective-permute-done | bytes 131104 | tf_op jit(solution)/shard_map/ppermute | solution.py:178
  41.5 2.9 %collective-permute-done.3.rest_2_ = bf16[8,64,128]{2,1,0:T(8,128)(2,1)S(1)} collective-permute-done((bf16[8,64,128]{2,1,0:T(8,128)(2,1)S(1)}, bf16[8,64,128]{2,1,0:T(8,128)(2,1)S(1)}, u32[]{:S(2)}, u32[]{:S(2)}) %collective-permute-start.3) | collective-permute-done | bytes 131104 | tf_op jit(solution)/shard_map/ppermute | solution.py:178
  44.5 5.1 %first_step.1 = (bf16[80,64,128]{2,1,0:T(8,128)(2,1)S(1)}, bf16[16,64,128]{2,1,0:T(8,128)(2,1)S(1)}, bf16[2048,128]{1,0:T(8,128)(2,1)S(1)}, bf16[32,64,1024]{2,1,0:T(8,128)(2,1)S(1)}) custom-call(s32[1]{0:T(128)S(6)} %copy.17.count, s32[16,32]{1,0:T(8,128)} %bitcast.12, s32[4,8]{1,0:T(4,128)} %bitcast.8, s32[4,32]{1,0:T(4,128)} %bitcast.16, ...), custom_call_target="tpu_custom_call" | custom-call | tf_op jit(solution)/shard_map/first_step/pallas_call | solution.py:328
  49.7 1.5 %collective-permute-done.6.passed = bf16[16,64,128]{2,1,0:T(8,128)(2,1)S(1)} collective-permute-done((bf16[16,64,128]{2,1,0:T(8,128)(2,1)S(1)}, bf16[16,64,128]{2,1,0:T(8,128)(2,1)S(1)}, u32[]{:S(2)}, u32[]{:S(2)}) %collective-permute-start.6) | collective-permute-done | bytes 262176 | tf_op jit(solution)/shard_map/ppermute | solution.py:172
  51.2 0.6 repack.3
  51.9 1.4 %collective-permute-start.7 = (bf16[8,64,128]{2,1,0:T(8,128)(2,1)S(1)}, bf16[8,64,128]{2,1,0:T(8,128)(2,1)S(1)}, u32[]{:S(2)}, u32[]{:S(2)}) collective-permute-start(bf16[8,64,128]{2,1,0:T(8,128)(2,1)S(1)} %get-tuple-element.29), channel_id=1, source_target_pairs={{0,2},{1,3},{2,0},{3,1},{4,6},{5,7},{6,4},{7,5},{8,10},{9,11},{10,... | collective-permute-start | bytes 393224 | tf_op jit(solution)/shard_map/ppermute | solution.py:178
  53.3 2.1 %collective-permute-start.8 = (bf16[8,64,128]{2,1,0:T(8,128)(2,1)S(1)}, bf16[8,64,128]{2,1,0:T(8,128)(2,1)S(1)}, u32[]{:S(2)}, u32[]{:S(2)}) collective-permute-start(bf16[8,64,128]{2,1,0:T(8,128)(2,1)S(1)} %get-tuple-element.30), channel_id=1, source_target_pairs={{0,6},{1,7},{2,4},{3,5},{4,2},{5,3},{6,0},{7,1},{8,14},{9,15},{10,... | collective-permute-start | bytes 393224 | tf_op jit(solution)/shard_map/ppermute | solution.py:178
  55.4 0.7 collective-permute-start.9
  56.1 1.6 %collective-permute-start.10 = (bf16[8,64,128]{2,1,0:T(8,128)(2,1)S(1)}, bf16[8,64,128]{2,1,0:T(8,128)(2,1)S(1)}, u32[]{:S(2)}, u32[]{:S(2)}) collective-permute-start(bf16[8,64,128]{2,1,0:T(8,128)(2,1)S(1)} %get-tuple-element.32), channel_id=1, source_target_pairs={{0,8},{8,16},{16,24},{24,32},{32,40},{40,48},{48,56},{56,64},{64,7... | collective-permute-start | bytes 393224 | tf_op jit(solution)/shard_map/ppermute | solution.py:185
  57.7 4.1 %collective-permute-start.11 = (bf16[8,64,128]{2,1,0:T(8,128)(2,1)S(1)}, bf16[8,64,128]{2,1,0:T(8,128)(2,1)S(1)}, u32[]{:S(2)}, u32[]{:S(2)}) collective-permute-start(bf16[8,64,128]{2,1,0:T(8,128)(2,1)S(1)} %get-tuple-element.33), channel_id=1, source_target_pairs={{0,120},{8,0},{16,8},{24,16},{32,24},{40,32},{48,40},{56,48},{64,5... | collective-permute-start | bytes 393224 | tf_op jit(solution)/shard_map/ppermute | solution.py:185
  61.8 0.8 %collective-permute-done.8.rest_1_ = bf16[8,64,128]{2,1,0:T(8,128)(2,1)S(1)} collective-permute-done((bf16[8,64,128]{2,1,0:T(8,128)(2,1)S(1)}, bf16[8,64,128]{2,1,0:T(8,128)(2,1)S(1)}, u32[]{:S(2)}, u32[]{:S(2)}) %collective-permute-start.8) | collective-permute-done | bytes 131104 | tf_op jit(solution)/shard_map/ppermute | solution.py:178
  62.6 2.1 %collective-permute-done.10.rest_3_ = bf16[8,64,128]{2,1,0:T(8,128)(2,1)S(1)} collective-permute-done((bf16[8,64,128]{2,1,0:T(8,128)(2,1)S(1)}, bf16[8,64,128]{2,1,0:T(8,128)(2,1)S(1)}, u32[]{:S(2)}, u32[]{:S(2)}) %collective-permute-start.10) | collective-permute-done | bytes 131104 | tf_op jit(solution)/shard_map/ppermute | solution.py:185
  64.7 3.9 %second_step.1 = (bf16[80,64,128]{2,1,0:T(8,128)(2,1)S(1)}, bf16[32,64,128]{2,1,0:T(8,128)(2,1)}) custom-call(s32[16,32]{1,0:T(8,128)S(1)} %bitcast.13, s32[1]{0:T(128)S(6)} %copy.17.count, bf16[32,64,1024]{2,1,0:T(8,128)(2,1)S(1)} %get-tuple-element.25.weights, bf16[2048,128]{1,0:T(8,128)(2,1)S(1)} %get-tuple-element.26.interp, ...), custom_call_target="tpu_custom_call", output_to_operand_aliasing={{0}: (8, {})} | custom-call | tf_op jit(solution)/shard_map/second_step/pallas_call | solution.py:386
  (26 shorter events, 0.2 us)
Async XLA Ops:
  2.3 42.1 %all-to-all-start = ((bf16[128,64,128]{2,1,0:T(8,128)(2,1)}), bf16[128,64,128]{2,1,0:T(8,128)(2,1)S(1)}, u32[]{:S(2)}, u32[]{:S(2)}) async-start(bf16[128,64,128]{2,1,0:T(8,128)(2,1)} %pick.1.after), calls=%async_computation | async-start | bytes 4194304 | tf_op jit(solution)/shard_map/all_to_all | solution.py:422
  13.5 3.5 %copy-start = (bf16[32,64,128]{2,1,0:T(8,128)(2,1)S(1)}, bf16[32,64,128]{2,1,0:T(8,128)(2,1)}, u32[]{:S(2)}) copy-start(bf16[32,64,128]{2,1,0:T(8,128)(2,1)} %latent.5) | copy-start | bytes 1572868
  13.5 3.5 %copy-start.3 = (s32[1,8,4]{1,2,0:T(4,128)S(1)}, s32[1,8,4]{1,2,0:T(4,128)}, u32[]{:S(2)}) copy-start(s32[1,8,4]{1,2,0:T(4,128)} %param.21) | copy-start | bytes 388
  13.5 3.5 %copy-start.8 = (s32[1,2,8]{2,1,0:T(2,128)S(1)}, s32[1,2,8]{2,1,0:T(2,128)}, u32[]{:S(2)}) copy-start(s32[1,2,8]{2,1,0:T(2,128)} %param.22) | copy-start | bytes 196
  15.4 1.6 %collective-permute-start = (bf16[16,64,128]{2,1,0:T(8,128)(2,1)S(1)}, bf16[16,64,128]{2,1,0:T(8,128)(2,1)S(1)}, u32[]{:S(2)}, u32[]{:S(2)}) collective-permute-start(bf16[16,64,128]{2,1,0:T(8,128)(2,1)S(1)} %first_hop.1), channel_id=1, source_target_pairs={{0,1},{1,0},{2,3},{3,2},{4,5},{5,4},{6,7},{7,6},{8,9},{9,8},{10,11... | collective-permute-start | bytes 786440 | tf_op jit(solution)/shard_map/ppermute | solution.py:172
  17.7 22.9 %collective-permute-start.1 = (bf16[8,64,128]{2,1,0:T(8,128)(2,1)S(1)}, bf16[8,64,128]{2,1,0:T(8,128)(2,1)S(1)}, u32[]{:S(2)}, u32[]{:S(2)}) collective-permute-start(bf16[8,64,128]{2,1,0:T(8,128)(2,1)S(1)} %get-tuple-element.20), channel_id=1, source_target_pairs={{0,2},{1,3},{2,0},{3,1},{4,6},{5,7},{6,4},{7,5},{8,10},{9,11},{10,... | collective-permute-start | bytes 393224 | tf_op jit(solution)/shard_map/ppermute | solution.py:178
  18.7 22.7 %collective-permute-start.2 = (bf16[8,64,128]{2,1,0:T(8,128)(2,1)S(1)}, bf16[8,64,128]{2,1,0:T(8,128)(2,1)S(1)}, u32[]{:S(2)}, u32[]{:S(2)}) collective-permute-start(bf16[8,64,128]{2,1,0:T(8,128)(2,1)S(1)} %get-tuple-element.21), channel_id=1, source_target_pairs={{0,6},{1,7},{2,4},{3,5},{4,2},{5,3},{6,0},{7,1},{8,14},{9,15},{10,... | collective-permute-start | bytes 393224 | tf_op jit(solution)/shard_map/ppermute | solution.py:178
  20.8 23.6 %collective-permute-start.3 = (bf16[8,64,128]{2,1,0:T(8,128)(2,1)S(1)}, bf16[8,64,128]{2,1,0:T(8,128)(2,1)S(1)}, u32[]{:S(2)}, u32[]{:S(2)}) collective-permute-start(bf16[8,64,128]{2,1,0:T(8,128)(2,1)S(1)} %get-tuple-element.22), channel_id=1, source_target_pairs={{0,4},{1,5},{2,6},{3,7},{4,0},{5,1},{6,2},{7,3},{8,12},{9,13},{10,... | collective-permute-start | bytes 393224 | tf_op jit(solution)/shard_map/ppermute | solution.py:178
  21.9 22.5 %collective-permute-start.4 = (bf16[8,64,128]{2,1,0:T(8,128)(2,1)S(1)}, bf16[8,64,128]{2,1,0:T(8,128)(2,1)S(1)}, u32[]{:S(2)}, u32[]{:S(2)}) collective-permute-start(bf16[8,64,128]{2,1,0:T(8,128)(2,1)S(1)} %get-tuple-element.23), channel_id=1, source_target_pairs={{0,8},{8,16},{16,24},{24,32},{32,40},{40,48},{48,56},{56,64},{64,7... | collective-permute-start | bytes 393224 | tf_op jit(solution)/shard_map/ppermute | solution.py:185
  23.0 21.4 %collective-permute-start.5 = (bf16[8,64,128]{2,1,0:T(8,128)(2,1)S(1)}, bf16[8,64,128]{2,1,0:T(8,128)(2,1)S(1)}, u32[]{:S(2)}, u32[]{:S(2)}) collective-permute-start(bf16[8,64,128]{2,1,0:T(8,128)(2,1)S(1)} %get-tuple-element.24), channel_id=1, source_target_pairs={{0,120},{8,0},{16,8},{24,16},{32,24},{40,32},{48,40},{56,48},{64,5... | collective-permute-start | bytes 393224 | tf_op jit(solution)/shard_map/ppermute | solution.py:185
  44.4 6.8 %copy-start.4 = (s32[1,8,4]{1,2,0:T(4,128)S(1)}, s32[1,8,4]{1,2,0:T(4,128)}, u32[]{:S(2)}) copy-start(s32[1,8,4]{1,2,0:T(4,128)} %param.21) | copy-start | bytes 388
  44.4 20.3 %copy-start.1 = (bf16[2,384,128]{2,1,0:T(8,128)(2,1)S(1)}, bf16[2,384,128]{2,1,0:T(8,128)(2,1)}, u32[]{:S(2)}) copy-start(bf16[2,384,128]{2,1,0:T(8,128)(2,1)} %w_in.3) | copy-start | bytes 589828
  44.4 20.3 %copy-start.2 = (bf16[2,128,128]{2,1,0:T(8,128)(2,1)S(1)}, bf16[2,128,128]{2,1,0:T(8,128)(2,1)}, u32[]{:S(2)}) copy-start(bf16[2,128,128]{2,1,0:T(8,128)(2,1)} %w_out.3) | copy-start | bytes 196612
  44.4 20.3 %copy-start.5 = (s32[32,16]{0,1:T(8,128)S(1)}, s32[32,16]{0,1:T(8,128)}, u32[]{:S(2)}) copy-start(s32[32,16]{0,1:T(8,128)} %param.16) | copy-start | bytes 6148
  44.5 20.3 %copy-start.6 = (f32[2,128]{1,0:T(2,128)S(1)}, f32[2,128]{1,0:T(2,128)}, u32[]{:S(2)}) copy-start(f32[2,128]{1,0:T(2,128)} %b_in.3) | copy-start | bytes 3076
  44.5 20.3 %copy-start.7 = (f32[2,128]{1,0:T(2,128)S(1)}, f32[2,128]{1,0:T(2,128)}, u32[]{:S(2)}) copy-start(f32[2,128]{1,0:T(2,128)} %gain.3) | copy-start | bytes 3076
  49.6 1.6 %collective-permute-start.6 = (bf16[16,64,128]{2,1,0:T(8,128)(2,1)S(1)}, bf16[16,64,128]{2,1,0:T(8,128)(2,1)S(1)}, u32[]{:S(2)}, u32[]{:S(2)}) collective-permute-start(bf16[16,64,128]{2,1,0:T(8,128)(2,1)S(1)} %get-tuple-element.28), channel_id=1, source_target_pairs={{0,1},{1,0},{2,3},{3,2},{4,5},{5,4},{6,7},{7,6},{8,9},{9,8},{10,11... | collective-permute-start | bytes 786440 | tf_op jit(solution)/shard_map/ppermute | solution.py:172
  51.9 9.9 %collective-permute-start.7 = (bf16[8,64,128]{2,1,0:T(8,128)(2,1)S(1)}, bf16[8,64,128]{2,1,0:T(8,128)(2,1)S(1)}, u32[]{:S(2)}, u32[]{:S(2)}) collective-permute-start(bf16[8,64,128]{2,1,0:T(8,128)(2,1)S(1)} %get-tuple-element.29), channel_id=1, source_target_pairs={{0,2},{1,3},{2,0},{3,1},{4,6},{5,7},{6,4},{7,5},{8,10},{9,11},{10,... | collective-permute-start | bytes 393224 | tf_op jit(solution)/shard_map/ppermute | solution.py:178
  53.3 9.3 %collective-permute-start.8 = (bf16[8,64,128]{2,1,0:T(8,128)(2,1)S(1)}, bf16[8,64,128]{2,1,0:T(8,128)(2,1)S(1)}, u32[]{:S(2)}, u32[]{:S(2)}) collective-permute-start(bf16[8,64,128]{2,1,0:T(8,128)(2,1)S(1)} %get-tuple-element.30), channel_id=1, source_target_pairs={{0,6},{1,7},{2,4},{3,5},{4,2},{5,3},{6,0},{7,1},{8,14},{9,15},{10,... | collective-permute-start | bytes 393224 | tf_op jit(solution)/shard_map/ppermute | solution.py:178
  55.4 7.2 %collective-permute-start.9 = (bf16[8,64,128]{2,1,0:T(8,128)(2,1)S(1)}, bf16[8,64,128]{2,1,0:T(8,128)(2,1)S(1)}, u32[]{:S(2)}, u32[]{:S(2)}) collective-permute-start(bf16[8,64,128]{2,1,0:T(8,128)(2,1)S(1)} %get-tuple-element.31), channel_id=1, source_target_pairs={{0,4},{1,5},{2,6},{3,7},{4,0},{5,1},{6,2},{7,3},{8,12},{9,13},{10,... | collective-permute-start | bytes 393224 | tf_op jit(solution)/shard_map/ppermute | solution.py:178
  56.1 8.6 %collective-permute-start.10 = (bf16[8,64,128]{2,1,0:T(8,128)(2,1)S(1)}, bf16[8,64,128]{2,1,0:T(8,128)(2,1)S(1)}, u32[]{:S(2)}, u32[]{:S(2)}) collective-permute-start(bf16[8,64,128]{2,1,0:T(8,128)(2,1)S(1)} %get-tuple-element.32), channel_id=1, source_target_pairs={{0,8},{8,16},{16,24},{24,32},{32,40},{40,48},{48,56},{56,64},{64,7... | collective-permute-start | bytes 393224 | tf_op jit(solution)/shard_map/ppermute | solution.py:185
  57.7 7.0 %collective-permute-start.11 = (bf16[8,64,128]{2,1,0:T(8,128)(2,1)S(1)}, bf16[8,64,128]{2,1,0:T(8,128)(2,1)S(1)}, u32[]{:S(2)}, u32[]{:S(2)}) collective-permute-start(bf16[8,64,128]{2,1,0:T(8,128)(2,1)S(1)} %get-tuple-element.33), channel_id=1, source_target_pairs={{0,120},{8,0},{16,8},{24,16},{32,24},{40,32},{48,40},{56,48},{64,5... | collective-permute-start | bytes 393224 | tf_op jit(solution)/shard_map/ppermute | solution.py:185

commit v5 on v3

--- a/solution.py
+++ b/solution.py
@@ -13,6 +13,7 @@
 VMEM = pl.BlockSpec(memory_space=pltpu.VMEM)
 ANY = pl.BlockSpec(memory_space=pl.ANY)
 CORES = 2
+WAYS = (1, 3, 2)
 
 
 def in_hbm(array):
@@ -70,7 +71,7 @@
     slots = sub_ids.shape[0]
     me = lax.axis_index("sub")
     mine = (me % CORES) * slots
-    for way, out in enumerate(outs, 1):
+    for way, out in zip(WAYS, outs):
         for slot in range(slots):
             out[mine + slot] = latent[sub_ids[slot, me ^ (way * CORES)]]
             out[slots - mine + slot] = passed[way * slots + slot]
@@ -174,7 +175,7 @@
     size = lax.axis_size("sub")
     return [
         lax.ppermute(piece, "sub", [(i, i ^ (way * CORES)) for i in range(size)])
-        for way, piece in enumerate(pieces, 1)
+        for way, piece in zip(WAYS, pieces)
     ]
 
 
@@ -193,7 +194,7 @@
     slots, peers = sub_ids.shape
     me = lax.axis_index("sub")
     pool[pl.ds(own + (me ^ 1) * slots, slots)] = passed[:slots]
-    for way, piece in enumerate(pieces, 1):
+    for way, piece in zip(WAYS, pieces):
         first = own + (me // CORES ^ way) * CORES * slots
         pool[pl.ds(first, piece.shape[0])] = piece[...]
     end = own + peers * slots

time: 71.2 us -> 70.6 us (level)
  starting transfers between devices: 31.5 us -> 30.3 us
    ppermute x6, starting transfers between devices: 9.48 us -> 8.27 us  [along_x(): lax.ppermute(piece, 'sub', [(i, i ^ way * CORES) for i in range(size)])]
where the time goes in v5:
time: 70.6 us; the launch traced here: 70.1 us
  starting transfers between devices  30.3 us (43%)
  waiting for transfers between devices  21.9 us (31%)
  Pallas kernels  17.1 us (24%)
  between operations  0.8 us (1%)
    all_to_all x1, waiting for transfers between devices, per_device(): lax.all_to_all(payload, ('dom', 'sub'), split_axis=0, concat_axis=0, tile...  15.9 us
    all_to_all x1, starting transfers between devices, per_device(): lax.all_to_all(payload, ('dom', 'sub'), split_axis=0, concat_axis=0, tile...  11.1 us
    ppermute x4, starting transfers between devices, along_dom(): lax.ppermute(blocks, 'dom', [(i, (i + distance) % size) for i in range(si...  10.7 us
    ppermute x6, starting transfers between devices, along_x(): lax.ppermute(piece, 'sub', [(i, i ^ way * CORES) for i in range(size)])  8.27 us
    pallas_call x1, Pallas kernels, second_step(): pl.pallas_call(second_kernel, in_specs=[SMEM] * 2 + [VMEM] * 7 + [ANY] +...  3.91 us
    pallas_call x1, Pallas kernels, prepare(): pl.pallas_call(prepare_kernel, in_specs=[ANY, VMEM] + [ANY] * 7, out_spec...  3.76 us
    pallas_call x1, Pallas kernels, first_step(): pl.pallas_call(first_kernel, in_specs=[SMEM] * 3 + [VMEM] * (7 + len(halo...  3.3 us
    ppermute x2, waiting for transfers between devices, to_other_core(): lax.ppermute(blocks, 'sub', [(i, i ^ 1) for i in range(lax.axis_size('sub...  3.04 us
  transfers between devices with their start and end apart: 13, of which 5 were waited for; matrix products, arithmetic and copies ran while one was open for 0% of the time, Pallas kernels for 10%

profile of v5, /device:TPU:0, one launch (start us, length us, event | category | flops | bytes accessed | tf_op | source)
XLA Modules:
  0.0 70.1 jit_solution(11235611105410191378)
XLA Ops:
  0.0 2.3 %pick.1.after = bf16[128,64,128]{2,1,0:T(8,128)(2,1)} custom-call(s32[1,128]{1,0:T(1,128)} %bitcast.17, bf16[8,64,128]{2,1,0:T(8,128)(2,1)} %table.1), custom_call_target="tpu_custom_call" | custom-call | tf_op jit(solution)/shard_map/pick/pallas_call | solution.py:134
  2.3 11.1 %all-to-all-start = ((bf16[128,64,128]{2,1,0:T(8,128)(2,1)}), bf16[128,64,128]{2,1,0:T(8,128)(2,1)S(1)}, u32[]{:S(2)}, u32[]{:S(2)}) async-start(bf16[128,64,128]{2,1,0:T(8,128)(2,1)} %pick.1.after), calls=%async_computation | async-start | bytes 4194304 | tf_op jit(solution)/shard_map/all_to_all | solution.py:424
  13.5 1.9 %first_hop.1 = bf16[16,64,128]{2,1,0:T(8,128)(2,1)S(1)} custom-call(s32[4,8]{1,0:T(4,128)} %bitcast.7, bf16[32,64,128]{2,1,0:T(8,128)(2,1)} %latent.5, bf16[128,64,128]{2,1,0:T(8,128)(2,1)} %pick.1.after), custom_call_target="tpu_custom_call" | custom-call | tf_op jit(solution)/shard_map/first_hop/pallas_call | solution.py:100
  15.4 0.1 collective-permute-start
  15.5 1.5 %collective-permute-done.passed = bf16[16,64,128]{2,1,0:T(8,128)(2,1)S(1)} collective-permute-done((bf16[16,64,128]{2,1,0:T(8,128)(2,1)S(1)}, bf16[16,64,128]{2,1,0:T(8,128)(2,1)S(1)}, u32[]{:S(2)}, u32[]{:S(2)}) %collective-permute-start) | collective-permute-done | bytes 262176 | tf_op jit(solution)/shard_map/ppermute | solution.py:171
  17.0 1.3 %repack.2 = (bf16[8,64,128]{2,1,0:T(8,128)(2,1)}, bf16[8,64,128]{2,1,0:T(8,128)(2,1)S(1)}, bf16[8,64,128]{2,1,0:T(8,128)(2,1)S(1)}, bf16[8,64,128]{2,1,0:T(8,128)(2,1)S(1)}, bf16[8,64,128]{2,1,0:T(8,128)(2,1)S(1)}) custom-call(s32[4,8]{1,0:T(4,128)S(1)} %bitcast.8, s32[2,8]{1,0:T(2,128)S(1)} %bitcast.14, bf16[32,64,128]{2,1,0:T(8,128)(2,1)S(1)} %copy-done, ...), custom_call_target="tpu_custom_call" | custom-call | tf_op jit(solution)/shard_map/repack/pallas_call | solution.py:160
  18.3 1.0 %collective-permute-start.1 = (bf16[8,64,128]{2,1,0:T(8,128)(2,1)}, bf16[8,64,128]{2,1,0:T(8,128)(2,1)S(1)}, u32[]{:S(2)}, u32[]{:S(2)}) collective-permute-start(bf16[8,64,128]{2,1,0:T(8,128)(2,1)} %get-tuple-element.32), channel_id=1, source_target_pairs={{0,2},{1,3},{2,0},{3,1},{4,6},{5,7},{6,4},{7,5},{8,10},{9,11},{10,... | collective-permute-start | bytes 393224 | tf_op jit(solution)/shard_map/ppermute | solution.py:177
  19.3 2.1 %collective-permute-start.2 = (bf16[8,64,128]{2,1,0:T(8,128)(2,1)S(1)}, bf16[8,64,128]{2,1,0:T(8,128)(2,1)S(1)}, u32[]{:S(2)}, u32[]{:S(2)}) collective-permute-start(bf16[8,64,128]{2,1,0:T(8,128)(2,1)S(1)} %get-tuple-element.33), channel_id=1, source_target_pairs={{0,6},{1,7},{2,4},{3,5},{4,2},{5,3},{6,0},{7,1},{8,14},{9,15},{10,... | collective-permute-start | bytes 393224 | tf_op jit(solution)/shard_map/ppermute | solution.py:177
  21.4 1.1 %collective-permute-start.3 = (bf16[8,64,128]{2,1,0:T(8,128)(2,1)S(1)}, bf16[8,64,128]{2,1,0:T(8,128)(2,1)S(1)}, u32[]{:S(2)}, u32[]{:S(2)}) collective-permute-start(bf16[8,64,128]{2,1,0:T(8,128)(2,1)S(1)} %get-tuple-element.34), channel_id=1, source_target_pairs={{0,4},{1,5},{2,6},{3,7},{4,0},{5,1},{6,2},{7,3},{8,12},{9,13},{10,... | collective-permute-start | bytes 393224 | tf_op jit(solution)/shard_map/ppermute | solution.py:177
  22.4 1.2 %collective-permute-start.4 = (bf16[8,64,128]{2,1,0:T(8,128)(2,1)S(1)}, bf16[8,64,128]{2,1,0:T(8,128)(2,1)S(1)}, u32[]{:S(2)}, u32[]{:S(2)}) collective-permute-start(bf16[8,64,128]{2,1,0:T(8,128)(2,1)S(1)} %get-tuple-element.35), channel_id=1, source_target_pairs={{0,8},{8,16},{16,24},{24,32},{32,40},{40,48},{48,56},{56,64},{64,7... | collective-permute-start | bytes 393224 | tf_op jit(solution)/shard_map/ppermute | solution.py:184
  23.6 4.2 %collective-permute-start.5 = (bf16[8,64,128]{2,1,0:T(8,128)(2,1)S(1)}, bf16[8,64,128]{2,1,0:T(8,128)(2,1)S(1)}, u32[]{:S(2)}, u32[]{:S(2)}) collective-permute-start(bf16[8,64,128]{2,1,0:T(8,128)(2,1)S(1)} %get-tuple-element.36), channel_id=1, source_target_pairs={{0,120},{8,0},{16,8},{24,16},{32,24},{40,32},{48,40},{56,48},{64,5... | collective-permute-start | bytes 393224 | tf_op jit(solution)/shard_map/ppermute | solution.py:184
  28.4 15.9 %all-to-all-done.received = bf16[128,64,128]{2,1,0:T(8,128)(2,1)S(1)} async-done(((bf16[128,64,128]{2,1,0:T(8,128)(2,1)}), bf16[128,64,128]{2,1,0:T(8,128)(2,1)S(1)}, u32[]{:S(2)}, u32[]{:S(2)}) %all-to-all-start) | async-done | bytes 2097184 | tf_op jit(solution)/shard_map/all_to_all | solution.py:424
  44.4 3.8 %prepare.1 = (bf16[2048,128]{1,0:T(8,128)(2,1)S(1)}, bf16[32,64,1024]{2,1,0:T(8,128)(2,1)S(1)}, bf16[80,64,128]{2,1,0:T(8,128)(2,1)S(1)}, bf16[2,384,128]{2,1,0:...) custom-call(s32[4,32]{1,0:T(4,128)} %bitcast.16, ...), custom_call_target="tpu_custom_call" | custom-call | tf_op jit(solution)/shard_map/prepare/pallas_call | solution.py:293
  48.2 3.3 %first_step.1 = (bf16[80,64,128]{2,1,0:T(8,128)(2,1)S(1)}, bf16[16,64,128]{2,1,0:T(8,128)(2,1)S(1)}) custom-call(s32[1]{0:T(128)S(6)} %copy.19.count, s32[16,32]{1,0:T(8,128)S(1)} %bitcast.12, s32[4,8]{1,0:T(4,128)S(1)} %bitcast.9, bf16[32,64,1024]{2,1,0:T(8,128)(2,1)S(1)} %get-tuple-element.25.weights, ...), custom_call_target="tpu_custom_call", output_to_operand_aliasing={{0}: (9, {})} | custom-call | tf_op jit(solution)/shard_map/first_step/pallas_call | solution.py:342
  51.6 1.5 %collective-permute-done.6.passed = bf16[16,64,128]{2,1,0:T(8,128)(2,1)S(1)} collective-permute-done((bf16[16,64,128]{2,1,0:T(8,128)(2,1)S(1)}, bf16[16,64,128]{2,1,0:T(8,128)(2,1)S(1)}, u32[]{:S(2)}, u32[]{:S(2)}) %collective-permute-start.6) | collective-permute-done | bytes 262176 | tf_op jit(solution)/shard_map/ppermute | solution.py:171
  53.1 0.6 repack.3
  53.8 0.7 collective-permute-start.10
  54.4 0.5 collective-permute-start.11
  55.0 3.0 %collective-permute-start.7 = (bf16[8,64,128]{2,1,0:T(8,128)(2,1)S(1)}, bf16[8,64,128]{2,1,0:T(8,128)(2,1)S(1)}, u32[]{:S(2)}, u32[]{:S(2)}) collective-permute-start(bf16[8,64,128]{2,1,0:T(8,128)(2,1)S(1)} %get-tuple-element.39), channel_id=1, source_target_pairs={{0,4},{1,5},{2,6},{3,7},{4,0},{5,1},{6,2},{7,3},{8,12},{9,13},{10,... | collective-permute-start | bytes 393224 | tf_op jit(solution)/shard_map/ppermute | solution.py:177
  57.9 0.6 collective-permute-start.8
  58.5 4.7 %collective-permute-start.9 = (bf16[8,64,128]{2,1,0:T(8,128)(2,1)S(1)}, bf16[8,64,128]{2,1,0:T(8,128)(2,1)S(1)}, u32[]{:S(2)}, u32[]{:S(2)}) collective-permute-start(bf16[8,64,128]{2,1,0:T(8,128)(2,1)S(1)} %get-tuple-element.41), channel_id=1, source_target_pairs={{0,120},{8,0},{16,8},{24,16},{32,24},{40,32},{48,40},{56,48},{64,5... | collective-permute-start | bytes 393224 | tf_op jit(solution)/shard_map/ppermute | solution.py:184
  63.3 0.4 collective-permute-done.11.rest_4_
  63.7 2.5 %collective-permute-done.8.rest_1_ = bf16[8,64,128]{2,1,0:T(8,128)(2,1)S(1)} collective-permute-done((bf16[8,64,128]{2,1,0:T(8,128)(2,1)S(1)}, bf16[8,64,128]{2,1,0:T(8,128)(2,1)S(1)}, u32[]{:S(2)}, u32[]{:S(2)}) %collective-permute-start.8) | collective-permute-done | bytes 131104 | tf_op jit(solution)/shard_map/ppermute | solution.py:184
  66.2 3.9 %second_step.1 = (bf16[80,64,128]{2,1,0:T(8,128)(2,1)S(1)}, bf16[32,64,128]{2,1,0:T(8,128)(2,1)}) custom-call(s32[16,32]{1,0:T(8,128)S(1)} %bitcast.13, s32[1]{0:T(128)S(6)} %copy.19.count, bf16[32,64,1024]{2,1,0:T(8,128)(2,1)S(1)} %get-tuple-element.25.weights, bf16[2048,128]{1,0:T(8,128)(2,1)S(1)} %get-tuple-element.26.interp, ...), custom_call_target="tpu_custom_call", output_to_operand_aliasing={{0}: (8, {})} | custom-call | tf_op jit(solution)/shard_map/second_step/pallas_call | solution.py:388
  (17 shorter events, 0.1 us)
Async XLA Ops:
  2.3 42.0 %all-to-all-start = ((bf16[128,64,128]{2,1,0:T(8,128)(2,1)}), bf16[128,64,128]{2,1,0:T(8,128)(2,1)S(1)}, u32[]{:S(2)}, u32[]{:S(2)}) async-start(bf16[128,64,128]{2,1,0:T(8,128)(2,1)} %pick.1.after), calls=%async_computation | async-start | bytes 4194304 | tf_op jit(solution)/shard_map/all_to_all | solution.py:424
  13.5 3.5 %copy-start = (bf16[32,64,128]{2,1,0:T(8,128)(2,1)S(1)}, bf16[32,64,128]{2,1,0:T(8,128)(2,1)}, u32[]{:S(2)}) copy-start(bf16[32,64,128]{2,1,0:T(8,128)(2,1)} %latent.5) | copy-start | bytes 1572868
  13.5 3.5 %copy-start.1 = (s32[1,8,4]{1,2,0:T(4,128)S(1)}, s32[1,8,4]{1,2,0:T(4,128)}, u32[]{:S(2)}) copy-start(s32[1,8,4]{1,2,0:T(4,128)} %param.21) | copy-start | bytes 388
  13.5 3.5 %copy-start.3 = (s32[1,2,8]{2,1,0:T(2,128)S(1)}, s32[1,2,8]{2,1,0:T(2,128)}, u32[]{:S(2)}) copy-start(s32[1,2,8]{2,1,0:T(2,128)} %param.22) | copy-start | bytes 196
  15.4 1.6 %collective-permute-start = (bf16[16,64,128]{2,1,0:T(8,128)(2,1)S(1)}, bf16[16,64,128]{2,1,0:T(8,128)(2,1)S(1)}, u32[]{:S(2)}, u32[]{:S(2)}) collective-permute-start(bf16[16,64,128]{2,1,0:T(8,128)(2,1)S(1)} %first_hop.1), channel_id=1, source_target_pairs={{0,1},{1,0},{2,3},{3,2},{4,5},{5,4},{6,7},{7,6},{8,9},{9,8},{10,11... | collective-permute-start | bytes 786440 | tf_op jit(solution)/shard_map/ppermute | solution.py:171
  18.3 29.8 %collective-permute-start.1 = (bf16[8,64,128]{2,1,0:T(8,128)(2,1)}, bf16[8,64,128]{2,1,0:T(8,128)(2,1)S(1)}, u32[]{:S(2)}, u32[]{:S(2)}) collective-permute-start(bf16[8,64,128]{2,1,0:T(8,128)(2,1)} %get-tuple-element.32), channel_id=1, source_target_pairs={{0,2},{1,3},{2,0},{3,1},{4,6},{5,7},{6,4},{7,5},{8,10},{9,11},{10,... | collective-permute-start | bytes 393224 | tf_op jit(solution)/shard_map/ppermute | solution.py:177
  19.3 28.8 %collective-permute-start.2 = (bf16[8,64,128]{2,1,0:T(8,128)(2,1)S(1)}, bf16[8,64,128]{2,1,0:T(8,128)(2,1)S(1)}, u32[]{:S(2)}, u32[]{:S(2)}) collective-permute-start(bf16[8,64,128]{2,1,0:T(8,128)(2,1)S(1)} %get-tuple-element.33), channel_id=1, source_target_pairs={{0,6},{1,7},{2,4},{3,5},{4,2},{5,3},{6,0},{7,1},{8,14},{9,15},{10,... | collective-permute-start | bytes 393224 | tf_op jit(solution)/shard_map/ppermute | solution.py:177
  21.4 26.8 %collective-permute-start.3 = (bf16[8,64,128]{2,1,0:T(8,128)(2,1)S(1)}, bf16[8,64,128]{2,1,0:T(8,128)(2,1)S(1)}, u32[]{:S(2)}, u32[]{:S(2)}) collective-permute-start(bf16[8,64,128]{2,1,0:T(8,128)(2,1)S(1)} %get-tuple-element.34), channel_id=1, source_target_pairs={{0,4},{1,5},{2,6},{3,7},{4,0},{5,1},{6,2},{7,3},{8,12},{9,13},{10,... | collective-permute-start | bytes 393224 | tf_op jit(solution)/shard_map/ppermute | solution.py:177
  22.4 25.7 %collective-permute-start.4 = (bf16[8,64,128]{2,1,0:T(8,128)(2,1)S(1)}, bf16[8,64,128]{2,1,0:T(8,128)(2,1)S(1)}, u32[]{:S(2)}, u32[]{:S(2)}) collective-permute-start(bf16[8,64,128]{2,1,0:T(8,128)(2,1)S(1)} %get-tuple-element.35), channel_id=1, source_target_pairs={{0,8},{8,16},{16,24},{24,32},{32,40},{40,48},{48,56},{56,64},{64,7... | collective-permute-start | bytes 393224 | tf_op jit(solution)/shard_map/ppermute | solution.py:184
  23.6 24.6 %collective-permute-start.5 = (bf16[8,64,128]{2,1,0:T(8,128)(2,1)S(1)}, bf16[8,64,128]{2,1,0:T(8,128)(2,1)S(1)}, u32[]{:S(2)}, u32[]{:S(2)}) collective-permute-start(bf16[8,64,128]{2,1,0:T(8,128)(2,1)S(1)} %get-tuple-element.36), channel_id=1, source_target_pairs={{0,120},{8,0},{16,8},{24,16},{32,24},{40,32},{48,40},{56,48},{64,5... | collective-permute-start | bytes 393224 | tf_op jit(solution)/shard_map/ppermute | solution.py:184
  44.4 3.8 %copy-start.2 = (s32[32,16]{0,1:T(8,128)S(1)}, s32[32,16]{0,1:T(8,128)}, u32[]{:S(2)}) copy-start(s32[32,16]{0,1:T(8,128)} %param.16) | copy-start | bytes 6148
  51.5 1.6 %collective-permute-start.6 = (bf16[16,64,128]{2,1,0:T(8,128)(2,1)S(1)}, bf16[16,64,128]{2,1,0:T(8,128)(2,1)S(1)}, u32[]{:S(2)}, u32[]{:S(2)}) collective-permute-start(bf16[16,64,128]{2,1,0:T(8,128)(2,1)S(1)} %get-tuple-element.38), channel_id=1, source_target_pairs={{0,1},{1,0},{2,3},{3,2},{4,5},{5,4},{6,7},{7,6},{8,9},{9,8},{10,11... | collective-permute-start | bytes 786440 | tf_op jit(solution)/shard_map/ppermute | solution.py:171
  53.8 9.5 %collective-permute-start.10 = (bf16[8,64,128]{2,1,0:T(8,128)(2,1)S(1)}, bf16[8,64,128]{2,1,0:T(8,128)(2,1)S(1)}, u32[]{:S(2)}, u32[]{:S(2)}) collective-permute-start(bf16[8,64,128]{2,1,0:T(8,128)(2,1)S(1)} %get-tuple-element.42), channel_id=1, source_target_pairs={{0,2},{1,3},{2,0},{3,1},{4,6},{5,7},{6,4},{7,5},{8,10},{9,11},{10,... | collective-permute-start | bytes 393224 | tf_op jit(solution)/shard_map/ppermute | solution.py:177
  54.4 9.3 %collective-permute-start.11 = (bf16[8,64,128]{2,1,0:T(8,128)(2,1)S(1)}, bf16[8,64,128]{2,1,0:T(8,128)(2,1)S(1)}, u32[]{:S(2)}, u32[]{:S(2)}) collective-permute-start(bf16[8,64,128]{2,1,0:T(8,128)(2,1)S(1)} %get-tuple-element.43), channel_id=1, source_target_pairs={{0,6},{1,7},{2,4},{3,5},{4,2},{5,3},{6,0},{7,1},{8,14},{9,15},{10,... | collective-permute-start | bytes 393224 | tf_op jit(solution)/shard_map/ppermute | solution.py:177
  55.0 8.7 %collective-permute-start.7 = (bf16[8,64,128]{2,1,0:T(8,128)(2,1)S(1)}, bf16[8,64,128]{2,1,0:T(8,128)(2,1)S(1)}, u32[]{:S(2)}, u32[]{:S(2)}) collective-permute-start(bf16[8,64,128]{2,1,0:T(8,128)(2,1)S(1)} %get-tuple-element.39), channel_id=1, source_target_pairs={{0,4},{1,5},{2,6},{3,7},{4,0},{5,1},{6,2},{7,3},{8,12},{9,13},{10,... | collective-permute-start | bytes 393224 | tf_op jit(solution)/shard_map/ppermute | solution.py:177
  57.9 8.3 %collective-permute-start.8 = (bf16[8,64,128]{2,1,0:T(8,128)(2,1)S(1)}, bf16[8,64,128]{2,1,0:T(8,128)(2,1)S(1)}, u32[]{:S(2)}, u32[]{:S(2)}) collective-permute-start(bf16[8,64,128]{2,1,0:T(8,128)(2,1)S(1)} %get-tuple-element.40), channel_id=1, source_target_pairs={{0,8},{8,16},{16,24},{24,32},{32,40},{40,48},{48,56},{56,64},{64,7... | collective-permute-start | bytes 393224 | tf_op jit(solution)/shard_map/ppermute | solution.py:184
  58.5 7.7 %collective-permute-start.9 = (bf16[8,64,128]{2,1,0:T(8,128)(2,1)S(1)}, bf16[8,64,128]{2,1,0:T(8,128)(2,1)S(1)}, u32[]{:S(2)}, u32[]{:S(2)}) collective-permute-start(bf16[8,64,128]{2,1,0:T(8,128)(2,1)S(1)} %get-tuple-element.41), channel_id=1, source_target_pairs={{0,120},{8,0},{16,8},{24,16},{32,24},{40,32},{48,40},{56,48},{64,5... | collective-permute-start | bytes 393224 | tf_op jit(solution)/shard_map/ppermute | solution.py:184
